TPU v7x, 32 devices: a whole 2x2x4 slice. The times are simulated.
32 devices in a mesh: dp: 16 (over z, y, core), tm: 2 (over x).
Axes of the slice: x: 2, y: 2, z: 4, core: 2. Of those that a mesh axis runs over, the one named last changes fastest.
Arguments:
- frames_in: bfloat16 [16, 4, 10, 16, 512], P('dp', 'tm'), may hold values from -6 to 6
- cotangent: bfloat16 [16, 8, 10, 16, 512], P('dp', 'tm'), may hold values from -6 to 6
- w_spatial: bfloat16 [9, 512, 512], P(None, 'dp'), may hold values from -0.09375 to 0.09375
- w_temporal: bfloat16 [3, 512, 512], P(None, 'dp'), may hold values from -0.15625 to 0.15625
Outputs:
- decoded: bfloat16 [16, 8, 10, 16, 512], P('dp', 'tm')
- grad_input: bfloat16 [16, 4, 10, 16, 512], P('dp', 'tm')
- grad_spatial: float32 [9, 512, 512], P(None, 'dp')
- grad_temporal: float32 [3, 512, 512], P(None, 'dp')
All inputs are finite; a program needn't handle non-finite values.
Results may differ from a plain program's by a relative error of at most 0.0051.
Values may be sent and summed in bfloat16 or wider, within the bound.
A program may use at most 192 MiB of HBM per device.

v0:
```python
import math

import jax
import jax.numpy as jnp
from jax import lax
from jax.sharding import PartitionSpec as P

spatial_taps = [(row_shift, col_shift) for row_shift in range(3) for col_shift in range(3)]


def passed_along(value, axis, steps):
    count = lax.axis_size(axis)
    leading, last = (max(0, -steps), min(count, count - steps))
    return lax.ppermute(value, axis, [(source, source + steps) for source in range(leading, last)])


def contract_rows(left, right):
    return lax.dot_general(
        left, right, (((0,), (0,)), ((), ())), preferred_element_type=jnp.float32
    )


def contract_cols(left, right):
    return lax.dot_general(
        left, right, (((1,), (1,)), ((), ())), preferred_element_type=jnp.float32
    )


def silu_slope(value):
    sigmoid = jax.nn.sigmoid(value)
    return sigmoid * (1.0 + value * (1.0 - sigmoid))


def spatial_forward(padded_act, weight):
    height = padded_act.shape[1] - 2
    width = padded_act.shape[2] - 2
    total = jnp.float32(0.0)
    for position, (row_shift, col_shift) in enumerate(spatial_taps):
        window = padded_act[
            :, row_shift : row_shift + height, col_shift : col_shift + width
        ].reshape(-1, padded_act.shape[3])
        total = total + jnp.dot(window, weight[position], preferred_element_type=jnp.float32)
    return total


def spatial_transpose(grad_flat, weight, frames, height, width):
    result = jnp.zeros((frames, height + 2, width + 2, weight.shape[1]), jnp.float32)
    for position, (row_shift, col_shift) in enumerate(spatial_taps):
        part = contract_cols(grad_flat, weight[position]).reshape(
            frames, height, width, weight.shape[1]
        )
        result = result.at[:, row_shift : row_shift + height, col_shift : col_shift + width].add(
            part
        )
    return result[:, 1:-1, 1:-1]


def temporal_forward(stacked, weight, frames):
    total = jnp.float32(0.0)
    for lag_step in range(3):
        window = stacked[lag_step : lag_step + frames].reshape(-1, stacked.shape[3])
        total = total + jnp.dot(window, weight[lag_step], preferred_element_type=jnp.float32)
    return total


def temporal_transpose(grad_flat, weight, frames, height, width):
    total = jnp.zeros((frames + 2, height, width, weight.shape[1]), jnp.float32)
    for lag_step in range(3):
        part = contract_cols(grad_flat, weight[lag_step]).reshape(
            frames, height, width, weight.shape[1]
        )
        total = total + jnp.pad(part, ((lag_step, 2 - lag_step), (0, 0), (0, 0), (0, 0)))
    return total


def weight_grads(padded_act, stacked, grad_frames, upstream_frames, frames, height, width):
    columns = grad_frames.shape[-1]
    channels = padded_act.shape[-1]
    upstream_flat = upstream_frames.reshape(-1, columns)
    grad_t = jnp.stack(
        [
            contract_rows(
                stacked[lag_step : lag_step + frames].reshape(-1, channels), upstream_flat
            )
            for lag_step in range(3)
        ]
    )
    collected = []
    for row_shift, col_shift in spatial_taps:
        window = padded_act[
            :, row_shift : row_shift + height, col_shift : col_shift + width
        ].reshape(-1, channels)
        collected.append(contract_rows(window, grad_frames))
    return (jnp.stack(collected), grad_t)


def per_device(frames_in, cotangent, w_spatial, w_temporal):
    source = frames_in[0]
    upstream = cotangent[0]
    frames = 2 * source.shape[0]
    height, width, channels = (source.shape[1], source.shape[2], source.shape[3])
    voxels = frames * height * width
    first_device = lax.axis_index("tm") == 0
    upsampled = jnp.repeat(source, 2, axis=0)
    up_float = upsampled.astype(jnp.float32)
    activated = jax.nn.silu(up_float).astype(jnp.bfloat16)
    padded_act = jnp.pad(activated, ((0, 0), (1, 1), (1, 1), (0, 0)))
    columns = padded_act
    spatial_sum = spatial_forward(columns, lax.all_gather(w_spatial, "dp", axis=1, tiled=True))
    spatial_out = spatial_sum.reshape(frames, height, width, channels).astype(jnp.bfloat16)
    previous = passed_along(spatial_out[frames - 2 :], "tm", 1)
    previous = jnp.where(first_device, jnp.broadcast_to(spatial_out[:1], previous.shape), previous)
    stacked = jnp.concatenate([previous, spatial_out], axis=0)
    columns = stacked
    temporal_sum = temporal_forward(
        columns, lax.all_gather(w_temporal, "dp", axis=1, tiled=True), frames
    )
    decoded = (up_float + temporal_sum.reshape(frames, height, width, channels)).astype(
        jnp.bfloat16
    )
    following = passed_along(upstream[:2], "tm", -1)
    extended_flat = jnp.concatenate([upstream, following], axis=0).reshape(-1, channels)
    piece = lax.all_gather(w_temporal, "dp", axis=1, tiled=True)
    pad_grad = temporal_transpose(extended_flat, piece, frames + 2, height, width)
    inner = pad_grad[2 : frames + 2]
    edge = jnp.where(first_device, pad_grad[0] + pad_grad[1], jnp.zeros_like(pad_grad[0]))
    inner = inner.at[0].add(edge)
    inner_grad = inner.reshape(voxels, piece.shape[1])
    spatial_grad = inner_grad.astype(jnp.bfloat16)
    grad_s_local, grad_t_local = weight_grads(
        padded_act, stacked, spatial_grad, upstream, frames, height, width
    )
    owned_s, owned_t = (
        lax.psum_scatter(grad_s_local, "dp", scatter_dimension=1, tiled=True),
        lax.psum_scatter(grad_t_local, "dp", scatter_dimension=1, tiled=True),
    )
    summed_s, summed_t = lax.psum((owned_s, owned_t), "tm")
    piece = lax.all_gather(w_spatial, "dp", axis=1, tiled=True)
    act_flat = spatial_transpose(spatial_grad, piece, frames, height, width).reshape(
        voxels, piece.shape[1]
    )
    act_grad = act_flat.reshape(frames, height, width, channels)
    up_grad = upstream.astype(jnp.float32) + act_grad * silu_slope(up_float)
    grad_input = (
        up_grad.reshape(frames // 2, 2, height, width, channels).sum(axis=1).astype(jnp.bfloat16)
    )
    inverse = 1.0 / math.sqrt(lax.axis_size("dp") * lax.axis_size("tm") * voxels)
    return (decoded[None], grad_input[None], summed_s * inverse, summed_t * inverse)


def solution(mesh):
    return jax.shard_map(
        per_device,
        mesh=mesh,
        in_specs=(
            P("dp", "tm", None, None, None),
            P("dp", "tm", None, None, None),
            P(None, "dp", None),
            P(None, "dp", None),
        ),
        out_specs=(
            P("dp", "tm", None, None, None),
            P("dp", "tm", None, None, None),
            P(None, "dp", None),
            P(None, "dp", None),
        ),
        check_vma=False,
    )
```

profile of v0, /device:TPU:0, one launch (start us, length us, event | category | flops | bytes accessed | tf_op | source)
XLA Modules:
  0.0 358.8 jit_solution(2832543486772294320)
XLA Ops:
  13.9 2.3 pad_slice_fusion
  16.3 6.4 %collective-permute-done.1 = bf16[2,10,16,512]{3,2,1,0:T(8,128)(2,1)} collective-permute-done((bf16[2,10,16,512]{3,2,1,0:T(8,128)(2,1)}, bf16[2,10,16,512]{3,2,1,0:T(8,128)(2,1)}, u32[]{:S(2)}, u32[]{:S(2)}) %collective-permute-start.1) | collective-permute-done | bytes 327712 | tf_op jit(solution)/shard_map/ppermute | solution.py:14
  22.7 29.9 %all-gather.5.cloned.1.call-done = bf16[3,512,512]{2,1,0:T(8,128)(2,1)} async-done(((bf16[3,32,512]{2,1,0:T(8,128)(2,1)}), bf16[3,512,512]{2,1,0:T(8,128)(2,1)}) %all-gather.5.cloned.1.call-update) | async-done | bytes 1572880 | tf_op jit(solution)/shard_map/all_gather | solution.py:116
  52.6 2.0 fusion.38
  59.9 47.2 %all-gather.3.cloned.1.call-done = bf16[9,512,512]{2,1,0:T(8,128)(2,1)} async-done(((bf16[9,32,512]{2,1,0:T(8,128)(2,1)}), bf16[9,512,512]{2,1,0:T(8,128)(2,1)}) %all-gather.3.cloned.1.call-update) | async-done | bytes 4718608 | tf_op jit(solution)/shard_map/all_gather | solution.py:109
  117.0 3.4 collective-permute-start
  122.3 5.5 %collective-permute-done = bf16[2,10,16,512]{3,2,1,0:T(8,128)(2,1)S(1)} collective-permute-done((bf16[2,10,16,512]{3,2,1,0:T(8,128)(2,1)S(1)}, bf16[2,10,16,512]{3,2,1,0:T(8,128)(2,1)S(1)}, u32[]{:S(2)}, u32[]{:S(2)}) %collective-permute-start) | collective-permute-done | bytes 327712 | tf_op jit(solution)/shard_map/ppermute | solution.py:14
  129.9 1.9 pad_maximum_fusion
  150.5 4.0 %convolution_add_fusion.6 = f32[4,10,16,512]{3,2,1,0:T(8,128)} fusion(bf16[4,10,16,512]{3,2,1,0:T(8,128)(2,1)S(1)} %fusion.80, s32[]{:T(128)} %bitcast.41, s32[]{:T(128)} %bitcast.42, bf16[9,512,512]{2,1,0:T(8,128)(2,1)} %all-gather.3.cloned.1.call-done, f32[4,10,16,512]{3,2,1,0:T(8,128)S(1)} %fusion.30), kind=kOutput, calls=%fused_computation.22 | convolution fusion | flops 335872000 | bytes 3802112 | tf_op jit(solution)/shard_map/dot_general | solution.py:24
  154.5 10.4 %scatter-add.36 = f32[4,12,18,512]{3,2,1,0:T(8,128)S(1)} dynamic-update-slice(f32[4,12,18,512]{3,2,1,0:T(8,128)S(1)} %scatter-add.35, f32[4,10,16,512]{3,2,1,0:T(8,128)} %convolution_add_fusion.6, s32[]{:T(128)} %constant.301.clone.1, s32[]{:T(128)} %bitcast.41, s32[]{:T(128)} %bitcast.42, s32[]{:T(128)} %constant.301.clone.1) | dynamic-update-slice | bytes 2621444 | tf_op jit(solution)/shard_map/scatter-add | solution.py:52
  164.9 4.6 %add_select_fusion = f32[4,10,16,512]{3,2,1,0:T(8,128)} fusion(bf16[4,10,16,512]{3,2,1,0:T(8,128)(2,1)S(1)} %fusion.80, f32[4,12,18,512]{3,2,1,0:T(8,128)S(1)} %scatter-add.36, s32[]{:T(128)} %bitcast.45, s32[]{:T(128)} %bitcast.46, pred[]{:T(512)} %and_reduce_fusion, bf16[9,512,512]{2,1,0:T(8,128)(2,1)} %all-gather.3.cloned.1.call-done), kind=kOutput, calls=%fused_computation.13 | convolution fusion | flops 336199680 | bytes 3802624 | tf_op jit(solution)/shard_map/dot_general | solution.py:24
  169.5 10.3 %scatter-add.39 = f32[4,12,18,512]{3,2,1,0:T(8,128)S(1)} dynamic-update-slice(f32[4,12,18,512]{3,2,1,0:T(8,128)S(1)} %scatter-add.36, f32[4,10,16,512]{3,2,1,0:T(8,128)} %add_select_fusion, s32[]{:T(128)} %constant.301.clone.1, s32[]{:T(128)} %bitcast.45, s32[]{:T(128)} %bitcast.46, s32[]{:T(128)} %constant.301.clone.1) | dynamic-update-slice | bytes 2621444 | tf_op jit(solution)/shard_map/scatter-add | solution.py:52
  181.4 2.7 convolution_add_fusion.4
  184.1 9.0 %scatter-add.41 = f32[4,12,18,512]{3,2,1,0:T(8,128)S(1)} dynamic-update-slice(f32[4,12,18,512]{3,2,1,0:T(8,128)S(1)} %fusion.1, f32[4,10,16,512]{3,2,1,0:T(8,128)} %convolution_add_fusion.4, s32[]{:T(128)} %constant.301.clone.1, s32[]{:T(128)} %constant.309.clone.1, s32[]{:T(128)} %constant.309.clone.1, s32[]{:T(128)} %constant.301.clone.1) | dynamic-update-slice | bytes 2621444 | tf_op jit(solution)/shard_map/scatter-add | solution.py:52
  193.0 2.7 convolution_add_fusion.3
  195.7 9.0 %scatter-add.44 = f32[4,12,18,512]{3,2,1,0:T(8,128)S(1)} dynamic-update-slice(f32[4,12,18,512]{3,2,1,0:T(8,128)S(1)} %scatter-add.41, f32[4,10,16,512]{3,2,1,0:T(8,128)} %convolution_add_fusion.3, s32[]{:T(128)} %constant.301.clone.1, s32[]{:T(128)} %constant.309.clone.1, s32[]{:T(128)} %constant.306.clone.1, s32[]{:T(128)} %constant.301.clone.1) | dynamic-update-slice | bytes 2621444 | tf_op jit(solution)/shard_map/scatter-add | solution.py:52
  206.3 2.7 convolution_add_fusion.1
  209.0 9.1 %scatter-add.46 = f32[4,12,18,512]{3,2,1,0:T(8,128)S(1)} dynamic-update-slice(f32[4,12,18,512]{3,2,1,0:T(8,128)S(1)} %fusion, f32[4,10,16,512]{3,2,1,0:T(8,128)} %convolution_add_fusion.1, s32[]{:T(128)} %constant.301.clone.1, s32[]{:T(128)} %constant.306.clone.1, s32[]{:T(128)} %constant.309.clone.1, s32[]{:T(128)} %constant.301.clone.1) | dynamic-update-slice | bytes 2621444 | tf_op jit(solution)/shard_map/scatter-add | solution.py:52
  218.2 2.8 convolution_add_fusion
  220.9 9.0 %scatter-add.49 = f32[4,12,18,512]{3,2,1,0:T(8,128)S(1)} dynamic-update-slice(f32[4,12,18,512]{3,2,1,0:T(8,128)S(1)} %scatter-add.46, f32[4,10,16,512]{3,2,1,0:T(8,128)} %convolution_add_fusion, s32[]{:T(128)} %constant.301.clone.1, s32[]{:T(128)} %constant.306.clone.1, s32[]{:T(128)} %constant.306.clone.1, s32[]{:T(128)} %constant.301.clone.1) | dynamic-update-slice | bytes 2621444 | tf_op jit(solution)/shard_map/scatter-add | solution.py:52
  230.0 2.5 bitcast_reduce_fusion
  234.4 77.6 %reduce-scatter.3.cloned.1.call-done = f32[9,32,512]{2,1,0:T(8,128)} async-done(((f32[9,512,512]{2,1,0:T(8,128)}), f32[9,32,512]{2,1,0:T(8,128)}) %reduce-scatter.3.cloned.1.call-update) | async-done | bytes 589840 | tf_op jit(solution)/shard_map/reduce_scatter | solution.py:134
  315.4 33.2 %all-reduce.8.cloned.1.call-done = (f32[9,32,512]{2,1,0:T(8,128)}, f32[3,32,512]{2,1,0:T(8,128)}) async-done(((f32[9,32,512]{2,1,0:T(8,128)}, f32[3,32,512]{2,1,0:T(8,128)}), (f32[9,32,512]{2,1,0:T(8,128)}, f32[3,32,512]{2,1,0:T(8,128)})) %all-reduce.8.cloned.1.call-update) | async-done | bytes 786448 | tf_op jit(solution)/shard_map/psum | solution.py:137
  348.7 1.9 broadcast_multiply_fusion
  (107 shorter events, 54.4 us)
Async XLA Ops:
  7.2 5.6 %copy-start.20 = (bf16[1,2,10,16,512]{4,3,2,1,0:T(8,128)(2,1)S(1)}, bf16[1,2,10,16,512]{4,3,2,1,0:T(8,128)(2,1)}, u32[]{:S(2)}) copy-start(bf16[1,2,10,16,512]{4,3,2,1,0:T(8,128)(2,1)} %param.24) | copy-start | bytes 983044
  7.2 45.5 %all-gather.5.cloned.1.call-start = ((), (), s32[]{:S(2)}) async-start(), calls=%async_computation.3 | async-start | bytes 1671168 | tf_op jit(solution)/shard_map/all_gather | solution.py:116
  7.9 99.2 %all-gather.3.cloned.1.call-start = ((), (), s32[]{:S(2)}) async-start(), calls=%async_computation.2 | async-start | bytes 5013504 | tf_op jit(solution)/shard_map/all_gather | solution.py:109
  8.7 225.7 %reduce-scatter.5.cloned.1.call-start = ((), (), s32[]{:S(2)}) async-start(), calls=%async_computation.5 | async-start | bytes 3342336 | tf_op jit(solution)/shard_map/reduce_scatter | solution.py:135
  10.4 12.3 %collective-permute-start.1 = (bf16[2,10,16,512]{3,2,1,0:T(8,128)(2,1)}, bf16[2,10,16,512]{3,2,1,0:T(8,128)(2,1)}, u32[]{:S(2)}, u32[]{:S(2)}) collective-permute-start(bf16[2,10,16,512]{3,2,1,0:T(8,128)(2,1)} %slice_bitcast_fusion), channel_id=1, source_target_pairs={{1,0},{3,2},{5,4},{7,6},{9,8},{11,10},{13,12},{15,14},{17,16},{19,... | collective-permute-start | bytes 983048 | tf_op jit(solution)/shard_map/ppermute | solution.py:14
  12.8 3.5 copy-start.5
  13.9 38.7 %copy-start = (bf16[1,4,10,16,512]{4,3,2,1,0:T(8,128)(2,1)S(1)}, bf16[1,4,10,16,512]{4,3,2,1,0:T(8,128)(2,1)}, u32[]{:S(2)}) copy-start(bf16[1,4,10,16,512]{4,3,2,1,0:T(8,128)(2,1)} %param.25) | copy-start | bytes 1966084
  52.6 2.0 copy-start.12
  58.3 1.5 copy-start.7
  107.2 1.7 copy-start.19
  107.2 3.3 copy-start.2
  108.9 1.6 copy-start.18
  110.5 1.1 copy-start.17
  112.7 1.1 copy-start.16
  116.9 10.8 %copy-start.3 = (bf16[640,512]{1,0:T(8,128)(2,1)}, bf16[640,512]{1,0:T(8,128)(2,1)S(1)}, u32[]{:S(2)}) copy-start(bf16[640,512]{1,0:T(8,128)(2,1)S(1)} %fusion.11) | copy-start | bytes 1966084
  117.0 10.8 %collective-permute-start = (bf16[2,10,16,512]{3,2,1,0:T(8,128)(2,1)S(1)}, bf16[2,10,16,512]{3,2,1,0:T(8,128)(2,1)S(1)}, u32[]{:S(2)}, u32[]{:S(2)}) collective-permute-start(bf16[2,10,16,512]{3,2,1,0:T(8,128)(2,1)S(1)} %bitcast.312), channel_id=1, source_target_pairs={{0,1},{2,3},{4,5},{6,7},{8,9},{10,11},{12,13},{14,15},{16,17},{18,... | collective-permute-start | bytes 983048 | tf_op jit(solution)/shard_map/ppermute | solution.py:14
  127.9 1.4 copy-start.10
  131.9 180.1 %reduce-scatter.3.cloned.1.call-start = ((), (), s32[]{:S(2)}) async-start(), calls=%async_computation.4 | async-start | bytes 10027008 | tf_op jit(solution)/shard_map/reduce_scatter | solution.py:134
  146.4 1.4 copy-start.22
  146.4 202.3 %all-reduce.8.cloned.1.call-start = ((), (), s32[]{:S(2)}) async-start(), calls=%async_computation.6 | async-start | bytes 1572864 | tf_op jit(solution)/shard_map/psum | solution.py:137
  220.9 9.1 %copy-start.1 = (bf16[1,4,10,16,512]{4,3,2,1,0:T(8,128)(2,1)S(1)}, bf16[1,4,10,16,512]{4,3,2,1,0:T(8,128)(2,1)}, u32[]{:S(2)}) copy-start(bf16[1,4,10,16,512]{4,3,2,1,0:T(8,128)(2,1)} %param.25) | copy-start | bytes 1966084
  230.0 2.5 copy-start.9
  232.5 79.5 %copy-start.11 = (bf16[4,10,16,512]{3,2,1,0:T(8,128)(2,1)S(1)}, bf16[4,10,16,512]{3,2,1,0:T(8,128)(2,1)}, u32[]{:S(2)}) copy-start(bf16[4,10,16,512]{3,2,1,0:T(8,128)(2,1)} %copy-done.10) | copy-start | bytes 1966084
  232.5 79.5 %copy-start.13 = (bf16[3,512,512]{2,1,0:T(8,128)(2,1)S(1)}, bf16[3,512,512]{2,1,0:T(8,128)(2,1)}, u32[]{:S(2)}) copy-start(bf16[3,512,512]{2,1,0:T(8,128)(2,1)} %all-gather.5.cloned.1.call-done) | copy-start | bytes 4718596
  (6 other events, 6.2 us)
Sparse Core Ops, SparseCore 0:
  10.2 42.3 all-gather.4
  54.8 52.2 all-gather.2
  132.0 65.6 reduce-scatter.4
  201.7 110.2 reduce-scatter.2
  314.4 34.2 all-reduce.7
where the time goes:
time: 362 us; the launch traced here: 359 us
  waiting for transfers between devices  201 us (56%)
  local copies, waits for them, and re-layouts  69 us (19%)
  matrix products  55.7 us (15%)
  between operations  14.3 us (4%)
  other arithmetic  13.4 us (4%)
  starting transfers between devices  5.05 us (1%)
    reduce_scatter x1, waiting for transfers between devices, per_device(): lax.psum_scatter(grad_s_local, 'dp', scatter_dimension=1, tiled=True)  77.6 us
    scatter-add x7, local copies, waits for them, and re-layouts, spatial_transpose(): result.at[:, row_shift:row_shift + height, col_shift:col_shift + width]  57.1 us
    all_gather x1, waiting for transfers between devices, per_device(): lax.all_gather(w_spatial, 'dp', axis=1, tiled=True)  47.2 us
    psum x1, waiting for transfers between devices, per_device(): summed_s, summed_t = lax.psum((owned_s, owned_t), 'tm')  33.2 us
    all_gather x1, waiting for transfers between devices, per_device(): lax.all_gather(w_temporal, 'dp', axis=1, tiled=True)  29.9 us
    dot_general x10, matrix products, contract_cols(): lax.dot_general(left, right, (((1,), (1,)), ((), ())), preferred_element_...  26.1 us
    dot_general x12, matrix products, contract_rows(): lax.dot_general(left, right, (((0,), (0,)), ((), ())), preferred_element_...  16.2 us
    ppermute x2, waiting for transfers between devices, passed_along(): lax.ppermute(value, axis, [(source, source + steps) for source in range(l...  11.9 us
  transfers between devices with their start and end apart: 7, of which 6 were waited for; matrix products, arithmetic and copies ran while one was open for 33% of the time, Pallas kernels for 0%

commit v1 on v0

--- a/solution.py
+++ b/solution.py
@@ -1,9 +1,16 @@
+import functools
 import math
 
 import jax
 import jax.numpy as jnp
 from jax import lax
+from jax.experimental import pallas as pl
+from jax.experimental.pallas import tpu as pltpu
 from jax.sharding import PartitionSpec as P
+
+MESH = pl.DeviceIdType.MESH
+LINE = 4
+PARTS = 4
 
 spatial_taps = [(row_shift, col_shift) for row_shift in range(3) for col_shift in range(3)]
 
@@ -148,21 +155,419 @@
     return (decoded[None], grad_input[None], summed_s * inverse, summed_t * inverse)
 
 
+def places(line, rows):
+    index = lax.axis_index("dp")
+    core = lax.rem(index, 2)
+    row = lax.rem(index // 2, rows)
+    return index // (2 * rows), row, core, lax.axis_index("tm")
+
+
+def block_of(line, row, core, rows):
+    return (line * rows + row) * 2 + core
+
+
+def greet(peers):
+    barrier = pltpu.get_barrier_semaphore()
+    for peer in peers:
+        pl.semaphore_signal(barrier, inc=1, device_id=peer, device_id_type=MESH)
+    pl.semaphore_wait(barrier, len(peers))
+
+
+def peers_of(line, row, core, tm, rows):
+    along = [
+        (block_of(lax.rem(line + step, LINE), row, core, rows), tm) for step in range(1, LINE)
+    ]
+    across = [
+        (block_of(line, lax.rem(row + step, rows), core, rows), tm) for step in range(1, rows)
+    ]
+    sibling = (block_of(line, row, 1 - core, rows), tm)
+    partner = (block_of(line, row, core, rows), 1 - tm)
+    return along, across, sibling, partner
+
+
+def gather_kernel(
+    rows, w_ref, u_ref, c_ref, w_all, u_all, c_all, send_sem, recv_sem, pair_send, pair_recv, own_sem
+):
+    line, row, core, tm = places(LINE, rows)
+    along, across, sibling, partner = peers_of(line, row, core, tm, rows)
+    greet(along + across + [sibling, partner])
+    taps = w_ref.shape[0] // PARTS
+    me = block_of(line, row, core, rows)
+    sent = []
+
+    def push(part, source, block, peer, slot):
+        copy = pltpu.make_async_remote_copy(
+            src_ref=source,
+            dst_ref=w_all.at[pl.ds(part * taps, taps), block],
+            send_sem=send_sem.at[part, slot],
+            recv_sem=recv_sem.at[part, block],
+            device_id=peer,
+            device_id_type=MESH,
+        )
+        copy.start()
+        sent.append(copy)
+
+    def landed(part, block):
+        view = w_all.at[pl.ds(part * taps, taps), block]
+        pltpu.make_async_copy(view, view, recv_sem.at[part, block]).wait()
+        return view
+
+    first_across = LINE - 1
+    first_core = first_across + LINE * (rows - 1)
+    for part in range(PARTS):
+        own = w_ref.at[pl.ds(part * taps, taps)]
+        for step, peer in enumerate(along):
+            push(part, own, me, peer, step)
+        for step, peer in enumerate(across):
+            push(part, own, me, peer, first_across + step)
+        push(part, own, me, sibling, first_core)
+    pairs = []
+    for number, (source, target) in enumerate(((u_ref, u_all), (c_ref, c_all))):
+        copy = pltpu.make_async_remote_copy(
+            src_ref=source,
+            dst_ref=target.at[tm],
+            send_sem=pair_send.at[number],
+            recv_sem=pair_recv.at[number],
+            device_id=partner,
+            device_id_type=MESH,
+        )
+        copy.start()
+        pairs.append(copy)
+    kept = [
+        pltpu.make_async_copy(w_ref, w_all.at[:, me], own_sem.at[0]),
+        pltpu.make_async_copy(u_ref, u_all.at[tm], own_sem.at[1]),
+        pltpu.make_async_copy(c_ref, c_all.at[tm], own_sem.at[2]),
+    ]
+    for copy in kept:
+        copy.start()
+
+    def relay_line(part):
+        for step in range(1, LINE):
+            block = block_of(lax.rem(line + step, LINE), row, core, rows)
+            view = landed(part, block)
+            for number, peer in enumerate(across):
+                push(part, view, block, peer, first_across + step * (rows - 1) + number)
+            push(part, view, block, sibling, first_core + step)
+
+    def relay_rows(part):
+        for number in range(1, rows):
+            for step in range(LINE):
+                block = block_of(
+                    lax.rem(line + step, LINE), lax.rem(row + number, rows), core, rows
+                )
+                view = landed(part, block)
+                push(part, view, block, sibling, first_core + number * LINE + step)
+
+    for part in range(PARTS):
+        relay_line(part)
+        if part:
+            relay_rows(part - 1)
+    relay_rows(PARTS - 1)
+    for part in range(PARTS):
+        for number in range(rows):
+            for step in range(LINE):
+                landed(part, block_of(step, number, 1 - core, rows))
+    for copy in sent:
+        copy.wait_send()
+    for copy in pairs:
+        copy.wait()
+    for copy in kept:
+        copy.wait()
+
+
+def gather(weights, source, upstream, devices):
+    rows = devices // (2 * LINE)
+    slots = (LINE - 1) + LINE * (rows - 1) + LINE * rows
+    anywhere = pl.BlockSpec(memory_space=pl.ANY)
+    taps, depth, columns = weights.shape
+    return pl.pallas_call(
+        functools.partial(gather_kernel, rows),
+        out_shape=(
+            jax.ShapeDtypeStruct((taps, devices, depth, columns), weights.dtype),
+            jax.ShapeDtypeStruct((2,) + source.shape, source.dtype),
+            jax.ShapeDtypeStruct((2,) + upstream.shape, upstream.dtype),
+        ),
+        in_specs=[anywhere] * 3,
+        out_specs=(anywhere,) * 3,
+        scratch_shapes=[
+            pltpu.SemaphoreType.DMA((PARTS, slots)),
+            pltpu.SemaphoreType.DMA((PARTS, devices)),
+            pltpu.SemaphoreType.DMA((2,)),
+            pltpu.SemaphoreType.DMA((2,)),
+            pltpu.SemaphoreType.DMA((3,)),
+        ],
+        compiler_params=pltpu.CompilerParams(collective_id=0, has_side_effects=True),
+        name="gather_weights",
+    )(weights, source, upstream)
+
+
+def reduce_kernel(
+    rows,
+    p_ref,
+    out_ref,
+    from_core,
+    to_row,
+    from_row,
+    to_line,
+    from_line,
+    core_send,
+    core_recv,
+    row_send,
+    row_recv,
+    line_send,
+    line_recv,
+    pair_send,
+    pair_recv,
+):
+    line, row, core, tm = places(LINE, rows)
+    along, across, sibling, partner = peers_of(line, row, core, tm, rows)
+    greet(along + across + [sibling, partner])
+
+    def push(source, target, send, recv, peer):
+        copy = pltpu.make_async_remote_copy(
+            src_ref=source,
+            dst_ref=target,
+            send_sem=send,
+            recv_sem=recv,
+            device_id=peer,
+            device_id_type=MESH,
+        )
+        copy.start()
+        return copy
+
+    wide = jnp.float32
+    sent = []
+    order = list(range(1, LINE)) + [0]
+    from_sibling = {}
+    for number in list(range(1, rows)) + [0]:
+        for step in order:
+            there = lax.rem(line + step, LINE)
+            beside = lax.rem(row + number, rows)
+            slot = number * LINE + step
+            copy = push(
+                p_ref.at[block_of(there, beside, 1 - core, rows)],
+                from_core.at[slot],
+                core_send.at[slot],
+                core_recv.at[slot],
+                sibling,
+            )
+            from_sibling[number, step] = copy
+    for number in range(1, rows):
+        for step in order:
+            there = lax.rem(line + step, LINE)
+            beside = lax.rem(row + number, rows)
+            slot = number * LINE + step
+            from_sibling[number, step].wait_recv()
+            to_row[slot] = (
+                p_ref[block_of(there, beside, core, rows)].astype(wide)
+                + from_core[slot].astype(wide)
+            ).astype(jnp.bfloat16)
+            sent.append(
+                push(
+                    to_row.at[slot],
+                    from_row.at[slot],
+                    row_send.at[slot],
+                    row_recv.at[slot],
+                    across[number - 1],
+                )
+            )
+    row_copies = {
+        (number, step): sent[(number - 1) * LINE + place]
+        for number in range(1, rows)
+        for place, step in enumerate(order)
+    }
+    line_copies = []
+    for step in order:
+        there = lax.rem(line + step, LINE)
+        from_sibling[0, step].wait_recv()
+        total = p_ref[block_of(there, row, core, rows)].astype(wide) + from_core[step].astype(wide)
+        for number in range(1, rows):
+            row_copies[number, step].wait_recv()
+            total = total + from_row[number * LINE + step].astype(wide)
+        if step:
+            to_line[step] = total.astype(jnp.bfloat16)
+            line_copies.append(
+                push(
+                    to_line.at[step],
+                    from_line.at[step],
+                    line_send.at[step],
+                    line_recv.at[step],
+                    along[step - 1],
+                )
+            )
+        else:
+            for copy in line_copies:
+                copy.wait_recv()
+            for other in range(1, LINE):
+                total = total + from_line[other].astype(wide)
+            out_ref[tm] = total.astype(jnp.bfloat16)
+    last = push(out_ref.at[tm], out_ref.at[tm], pair_send.at[0], pair_recv.at[0], partner)
+    for copy in list(from_sibling.values()) + sent + line_copies:
+        copy.wait_send()
+    last.wait()
+
+
+def reduce_grads(partial, devices):
+    rows = devices // (2 * LINE)
+    block = partial.shape[1:]
+    in_vmem = pl.BlockSpec(memory_space=pltpu.VMEM)
+    many = rows * LINE
+    return pl.pallas_call(
+        functools.partial(reduce_kernel, rows),
+        out_shape=jax.ShapeDtypeStruct((2,) + block, partial.dtype),
+        in_specs=[in_vmem],
+        out_specs=in_vmem,
+        scratch_shapes=[
+            pltpu.VMEM((many,) + block, partial.dtype),
+            pltpu.VMEM((many,) + block, partial.dtype),
+            pltpu.VMEM((many,) + block, partial.dtype),
+            pltpu.VMEM((LINE,) + block, partial.dtype),
+            pltpu.VMEM((LINE,) + block, partial.dtype),
+            pltpu.SemaphoreType.DMA((many,)),
+            pltpu.SemaphoreType.DMA((many,)),
+            pltpu.SemaphoreType.DMA((many,)),
+            pltpu.SemaphoreType.DMA((many,)),
+            pltpu.SemaphoreType.DMA((LINE,)),
+            pltpu.SemaphoreType.DMA((LINE,)),
+            pltpu.SemaphoreType.DMA((1,)),
+            pltpu.SemaphoreType.DMA((1,)),
+        ],
+        compiler_params=pltpu.CompilerParams(
+            collective_id=1, has_side_effects=True, vmem_limit_bytes=40 * 2**20
+        ),
+        name="reduce_grads",
+    )(partial)
+
+
+def beside(frames, direction):
+    edges = ((0, 0), (1, 1), (1, 1), (0, 0))
+    wide = jnp.pad(frames, edges)
+    cols = frames.shape[2]
+    shifts = (0, 1, 2) if direction > 0 else (2, 1, 0)
+    return jnp.concatenate([wide[:, :, s : s + cols] for s in shifts], axis=-1)
+
+
+def paired_device(frames_in, cotangent, w_spatial, w_temporal):
+    devices = lax.axis_size("dp")
+    tm = lax.axis_index("tm")
+    source = frames_in[0]
+    own, height, width, channels = source.shape
+    weights, sources, upstreams = gather(
+        jnp.concatenate([w_temporal, w_spatial], axis=0), source, cotangent[0], devices
+    )
+    weights = weights.reshape(weights.shape[0], channels, channels)
+    w_t, w_s = weights[:3], weights[3:]
+    clip = sources.reshape((2 * own, height, width, channels))
+    upstream = upstreams.reshape((4 * own, height * width, channels))
+    frames = 2 * own
+    even, odd = upstream[0::2], upstream[1::2]
+    nothing = jnp.zeros_like(even[:1])
+    even_next = jnp.concatenate([even[1:], nothing], axis=0)
+    odd_next = jnp.concatenate([odd[1:], nothing], axis=0)
+
+    def back(frame_list, weight):
+        return lax.dot_general(
+            frame_list, weight, (((2,), (1,)), ((), ())), preferred_element_type=jnp.float32
+        )
+
+    with jax.named_scope("temporal_back"):
+        first = (jnp.arange(frames) == 0)[:, None, None]
+        grads = (
+            back(even, w_t[2])
+            + back(odd, w_t[2])
+            + back(odd, w_t[1])
+            + back(even_next, w_t[1])
+            + back(even_next, w_t[0])
+            + back(odd_next, w_t[0])
+        )
+        edge = (
+            back(even[:1], w_t[0]) + back(odd[:1], w_t[0]) + back(even[:1], w_t[1])
+        )
+        grads = jnp.where(first, grads + edge, grads).astype(jnp.bfloat16)
+
+    with jax.named_scope("spatial"):
+        activated = jax.nn.silu(clip.astype(jnp.float32)).astype(jnp.bfloat16)
+        columns = beside(activated, 1)
+        spatial = jnp.float32(0.0)
+        for r in range(3):
+            spatial = spatial + jnp.dot(
+                columns[:, r : r + height].reshape(-1, 3 * channels),
+                w_s[3 * r : 3 * r + 3].reshape(3 * channels, channels),
+                preferred_element_type=jnp.float32,
+            )
+        spatial = spatial.astype(jnp.bfloat16).reshape(frames, height * width, channels)
+        before = jnp.concatenate([spatial[:1], spatial[:-1]], axis=0)
+
+    with jax.named_scope("weight_grads"):
+        half = channels // 2
+        start = tm * half
+        grads_half = lax.dynamic_slice_in_dim(grads, start, half, 2).reshape(-1, half)
+        even_half = lax.dynamic_slice_in_dim(even, start, half, 2).reshape(-1, half)
+        odd_half = lax.dynamic_slice_in_dim(odd, start, half, 2).reshape(-1, half)
+        both_half = jnp.concatenate([even_half, odd_half], axis=0)
+        now, past = spatial.reshape(-1, channels), before.reshape(-1, channels)
+        parts = [
+            contract_rows(jnp.concatenate([past, past], axis=0), both_half)[None],
+            contract_rows(jnp.concatenate([past, now], axis=0), both_half)[None],
+            contract_rows(jnp.concatenate([now, now], axis=0), both_half)[None],
+        ]
+        for r in range(3):
+            window = columns[:, r : r + height].reshape(-1, 3 * channels)
+            parts.append(contract_rows(window, grads_half).reshape(3, channels, half))
+        partial = jnp.concatenate(parts, axis=0).astype(jnp.bfloat16)
+        partial = partial.reshape(12, devices, channels // devices, half).transpose(1, 0, 2, 3)
+    summed = reduce_grads(partial, devices)
+
+    mine = own * tm
+    with jax.named_scope("temporal"):
+        now = lax.dynamic_slice_in_dim(spatial, mine, own, 0).reshape(-1, channels)
+        past = lax.dynamic_slice_in_dim(before, mine, own, 0).reshape(-1, channels)
+        held = source.astype(jnp.float32)
+        common = (
+            jnp.dot(past, w_t[0], preferred_element_type=jnp.float32)
+            + jnp.dot(now, w_t[2], preferred_element_type=jnp.float32)
+            + held.reshape(-1, channels)
+        )
+        ahead = common + jnp.dot(past, w_t[1], preferred_element_type=jnp.float32)
+        behind = common + jnp.dot(now, w_t[1], preferred_element_type=jnp.float32)
+        decoded = jnp.stack(
+            [
+                ahead.astype(jnp.bfloat16).reshape(own, height, width, channels),
+                behind.astype(jnp.bfloat16).reshape(own, height, width, channels),
+            ],
+            axis=1,
+        ).reshape(2 * own, height, width, channels)
+    with jax.named_scope("spatial_back"):
+        mine_grads = lax.dynamic_slice_in_dim(grads, mine, own, 0).reshape(
+            own, height, width, channels
+        )
+        spread = beside(mine_grads, -1)
+        act_grad = jnp.float32(0.0)
+        for r in range(3):
+            window = spread[:, 2 - r : 2 - r + height].reshape(-1, 3, channels)
+            act_grad = act_grad + lax.dot_general(
+                window,
+                w_s[3 * r : 3 * r + 3],
+                (((1, 2), (0, 2)), ((), ())),
+                preferred_element_type=jnp.float32,
+            )
+        act_grad = act_grad.reshape(own, height, width, channels)
+        pair = cotangent[0].reshape(own, 2, height, width, channels).astype(jnp.float32)
+        grad_input = (pair[:, 0] + pair[:, 1] + act_grad * silu_slope(held)).astype(jnp.bfloat16)
+
+    inverse = 1.0 / math.sqrt(devices * 2 * frames * height * width)
+    whole = jnp.concatenate([summed[0], summed[1]], axis=-1).astype(jnp.float32) * inverse
+    return (decoded[None], grad_input[None], whole[3:], whole[:3])
+
+
 def solution(mesh):
+    clip_split = P("dp", "tm", None, None, None)
+    rows_split = P(None, "dp", None)
+    paired = mesh.shape["tm"] == 2 and mesh.shape["dp"] % (2 * LINE) == 0
     return jax.shard_map(
-        per_device,
+        paired_device if paired else per_device,
         mesh=mesh,
-        in_specs=(
-            P("dp", "tm", None, None, None),
-            P("dp", "tm", None, None, None),
-            P(None, "dp", None),
-            P(None, "dp", None),
-        ),
-        out_specs=(
-            P("dp", "tm", None, None, None),
-            P("dp", "tm", None, None, None),
-            P(None, "dp", None),
-            P(None, "dp", None),
-        ),
+        in_specs=(clip_split, clip_split, rows_split, rows_split),
+        out_specs=(clip_split, clip_split, rows_split, rows_split),
         check_vma=False,
     )

time: 362 us -> 160 us (0.44)
  waiting for transfers between devices: 201 us -> 0 us
  Pallas kernels: 0 us -> 89 us
  local copies, waits for them, and re-layouts: 69 us -> 36.2 us
  matrix products: 55.7 us -> 25.7 us
  between operations: 14.3 us -> 1.09 us
  other arithmetic: 13.4 us -> 7.21 us
  starting transfers between devices: 5.05 us -> 0 us
    pallas_call x0 -> x2, Pallas kernels: none -> 89 us  [the longest x1 49.1 us: gather(): pl.pallas_call(functools.partial(gather_kernel, rows), out_shape=(jax.Sha...]
    reduce_scatter x2 -> x0, waiting for transfers between devices: 77.6 us -> none  [the longest x1 77.6 us: per_device(): lax.psum_scatter(grad_s_local, 'dp', scatter_dimension=1, tiled=True)]
    all_gather x2 -> x0, waiting for transfers between devices: 77.2 us -> none  [the longest x1 47.2 us: per_device(): lax.all_gather(w_spatial, 'dp', axis=1, tiled=True)]
    scatter-add x7 -> x0, local copies, waits for them, and re-layouts: 57.1 us -> none  [spatial_transpose(): result.at[:, row_shift:row_shift + height, col_shift:col_shift + width]]
    psum x1 -> x0, waiting for transfers between devices: 33.2 us -> none  [per_device(): summed_s, summed_t = lax.psum((owned_s, owned_t), 'tm')]
    dot_general x22 -> x19, matrix products: 35.8 us -> 18.8 us  [the longest x3 7.43 us: paired_device(): jnp.dot(columns[:, r:r + height].reshape(-1, 3 * channels), w_s[3 * r:3 *...]
    reshape x0 -> x6, local copies, waits for them, and re-layouts: none -> 16.5 us  [the longest x3 10.2 us: paired_device(): columns[:, r:r + height].reshape(-1, 3 * channels)]
    ppermute x2 -> x0, waiting for transfers between devices: 11.9 us -> none  [passed_along(): lax.ppermute(value, axis, [(source, source + steps) for source in range(l...]
  transfers between devices with their start and end apart: 7 -> 0, of which waited for: 6 -> 0; matrix products, arithmetic and copies ran while one was open for 33% -> 0% of each run, Pallas kernels for 0% -> 0%
where the time goes in v1:
time: 160 us; the launch traced here: 159 us
  Pallas kernels  89 us (56%)
  local copies, waits for them, and re-layouts  36.2 us (23%)
  matrix products  25.7 us (16%)
  other arithmetic  7.21 us (5%)
    pallas_call x1, Pallas kernels, gather(): pl.pallas_call(functools.partial(gather_kernel, rows), out_shape=(jax.Sha...  49.1 us
    pallas_call x1, Pallas kernels, reduce_grads(): pl.pallas_call(functools.partial(reduce_kernel, rows), out_shape=jax.Shap...  39.9 us
    reshape x3, local copies, waits for them, and re-layouts, paired_device(): columns[:, r:r + height].reshape(-1, 3 * channels)  10.2 us
    dot_general x3, matrix products, paired_device(): jnp.dot(columns[:, r:r + height].reshape(-1, 3 * channels), w_s[3 * r:3 *...  7.43 us
    dot_general x6, matrix products, contract_rows(): lax.dot_general(left, right, (((0,), (0,)), ((), ())), preferred_element_...  6.96 us
    reshape x3, local copies, waits for them, and re-layouts, paired_device(): window = spread[:, 2 - r:2 - r + height].reshape(-1, 3, channels)  6.25 us
    unnamed x45, local copies, waits for them, and re-layouts  6.13 us
    dot_general x3, matrix products, paired_device(): lax.dot_general(window, w_s[3 * r:3 * r + 3], (((1, 2), (0, 2)), ((), ())...  5.86 us

profile of v1, /device:TPU:0, one launch (start us, length us, event | category | flops | bytes accessed | tf_op | source)
XLA Modules:
  0.0 159.2 jit_solution(5339661709029222262)
XLA Ops:
  0.6 1.8 %pad_maximum_fusion.17.w_ref = bf16[12,32,512]{2,1,0:T(8,128)(2,1)} fusion(bf16[9,32,512]{2,1,0:T(8,128)(2,1)} %param.6, bf16[3,32,512]{2,1,0:T(8,128)(2,1)} %param.7), kind=kLoop, calls=%fused_computation.76 | loop fusion | flops 196608 | bytes 786432 | tf_op jit(solution)/shard_map/concatenate | solution.py:456
  2.4 2.3 %convert.31 = f32[2,2,10,16,512]{4,3,2,1,0:T(8,128)} convert(bf16[2,2,10,16,512]{4,3,2,1,0:T(8,128)(2,1)} %bitcast.155) | non-fusion elementwise | flops 327680 | bytes 1966080 | tf_op jit(solution)/shard_map/spatial_back/convert_element_type | solution.py:555
  4.7 49.1 %gather_weights.1 = (bf16[12,16,32,512]{3,2,1,0:T(8,128)(2,1)}, bf16[2,2,10,16,512]{4,3,2,1,0:T(8,128)(2,1)}, bf16[2,4,10,16,512]{4,3,2,1,0:T(8,128)(2,1)}) custom-call(bf16[12,32,512]{2,1,0:T(8,128)(2,1)} %pad_maximum_fusion.17.w_ref, bf16[2,10,16,512]{3,2,1,0:T(8,128)(2,1)} %bitcast.148, bf16[4,10,16,512]{3,2,1,0:T(8,128)(2,1)} %bitcast.156), custom_call_target="tpu_custom_call" | custom-call | tf_op jit(solution)/shard_map/gather_weights/pallas_call | solution.py:283
  53.8 1.6 fusion.32
  56.4 2.1 %fusion.61 = (bf16[1,16,32,512]{3,2,1,0:T(8,128)(2,1)S(1)}, bf16[1,16,32,512]{3,2,1,0:T(8,128)(2,1)S(1)}, bf16[1,16,32,512]{3,2,1,0:T(8,128)(2,1)S(1)}) fusion(bf16[12,16,32,512]{3,2,1,0:T(8,128)(2,1)} %get-tuple-element.8), kind=kLoop, calls=%fused_computation.100 | loop fusion | bytes 3145728 | tf_op jit(solution)/shard_map/temporal/slice | solution.py:531
  58.9 2.2 %fusion.62 = (bf16[3,16,32,512]{3,2,1,0:T(8,128)(2,1)}, bf16[3,16,32,512]{3,2,1,0:T(8,128)(2,1)}, bf16[3,16,32,512]{3,2,1,0:T(8,128)(2,1)S(1)}) fusion(bf16[12,16,32,512]{3,2,1,0:T(8,128)(2,1)S(1)} %copy-done.3), kind=kLoop, calls=%fused_computation.101 | loop fusion | bytes 9437184 | tf_op jit(solution)/shard_map/spatial/slice | solution.py:495
  66.8 1.8 %fusion.63 = (bf16[4,10,16,1536]{3,2,1,0:T(8,128)(2,1)}, bf16[4,10,16,1536]{3,2,1,0:T(8,128)(2,1)S(1)}, bf16[4,10,16,1536]{3,2,1,0:T(8,128)(2,1)S(1)}) fusion(bf16[4,12,16,1536]{3,2,1,0:T(8,128)(2,1)S(1)} %pad_maximum_fusion), kind=kLoop, calls=%fused_computation.102 | loop fusion | bytes 11796480 | tf_op jit(solution)/shard_map/spatial/slice | solution.py:494
  68.7 1.3 copy-done.2
  70.0 2.3 %fusion.66 = f32[640,512]{1,0:T(8,128)} fusion(bf16[640,1536]{1,0:T(8,128)(2,1)S(1)} %bitcast.142, bf16[1536,512]{1,0:T(8,128)(2,1)S(1)} %bitcast.144), kind=kOutput, calls=%fused_computation.105 | convolution fusion | flops 1006632960 | bytes 4849664 | tf_op jit(solution)/shard_map/spatial/dot_general | solution.py:493
  72.3 4.0 %copy.19 = bf16[640,1536]{0,1:T(8,128)(2,1)} copy(bf16[640,1536]{1,0:T(8,128)(2,1)} %bitcast.143) | data formatting | bytes 3932160 | tf_op jit(solution)/shard_map/spatial/reshape | solution.py:494
  76.3 3.1 %convolution_add_fusion.6 = f32[640,512]{1,0:T(8,128)S(1)} fusion(f32[640,512]{1,0:T(8,128)} %fusion.66, bf16[640,1536]{1,0:T(8,128)(2,1)S(1)} %bitcast.138, bf16[1536,512]{1,0:T(8,128)(2,1)} %bitcast.160), kind=kOutput, calls=%fused_computation.28 | convolution fusion | flops 1006960640 | bytes 6160384 | tf_op jit(solution)/shard_map/spatial/dot_general | solution.py:493
  79.4 2.0 %fusion.24 = bf16[640,512]{1,0:T(8,128)(2,1)} fusion(f32[640,512]{1,0:T(8,128)S(1)} %convolution_add_fusion.6, bf16[640,1536]{1,0:T(8,128)(2,1)S(1)} %bitcast.141, bf16[1536,512]{1,0:T(8,128)(2,1)S(1)} %bitcast.163), kind=kOutput, calls=%fused_computation.29 | convolution fusion | flops 1007288320 | bytes 5505024 | tf_op jit(solution)/shard_map/spatial/dot_general | solution.py:493
  81.4 4.0 %copy.23 = bf16[640,1536]{0,1:T(8,128)(2,1)} copy(bf16[640,1536]{1,0:T(8,128)(2,1)} %bitcast.140) | data formatting | bytes 3932160 | tf_op jit(solution)/shard_map/spatial/reshape | solution.py:494
  85.4 2.3 %copy.21 = bf16[640,1536]{0,1:T(8,128)(2,1)} copy(bf16[640,1536]{1,0:T(8,128)(2,1)S(1)} %bitcast.139) | data formatting | bytes 3932160 | tf_op jit(solution)/shard_map/spatial/reshape | solution.py:494
  88.6 2.1 %fusion.42 = bf16[512,256]{1,0:T(8,128)(2,1)S(1)} fusion(bf16[640,512]{1,0:T(8,128)(2,1)} %fusion.24, bf16[640,256]{1,0:T(8,128)(2,1)} %bitcast.174, bf16[640,256]{1,0:T(8,128)(2,1)} %bitcast.177), kind=kOutput, calls=%fused_computation.53 | convolution fusion | flops 339607552 | bytes 1572864 | tf_op jit(solution)/shard_map/weight_grads/dot_general | solution.py:25
  92.0 1.3 fusion.40
  93.2 1.3 fusion.41
  97.7 1.4 fusion.65
  99.1 3.1 %reshape.180 = bf16[320,3,512]{2,1,0:T(4,128)(2,1)S(1)} reshape(bf16[2,10,16,1536]{3,2,1,0:T(8,128)(2,1)} %get-tuple-element.21) | data formatting | bytes 1966080 | tf_op jit(solution)/shard_map/spatial_back/reshape | solution.py:547
  102.3 1.6 reshape.182
  103.8 2.5 %convolution_bitcast_fusion = f32[320,512]{1,0:T(8,128)S(1)} fusion(bf16[3,512,512]{2,1,0:T(8,128)(2,1)} %bitcast.162, bf16[320,3,512]{2,1,0:T(4,128)(2,1)} %reshape.182), kind=kOutput, calls=%fused_computation.44 | convolution fusion | flops 503316480 | bytes 3211264 | tf_op jit(solution)/shard_map/spatial_back/dot_general | solution.py:548
  106.3 1.6 reshape.181
  107.9 2.6 %convolution_bitcast_fusion.1 = f32[320,512]{1,0:T(8,128)S(1)} fusion(bf16[3,512,512]{2,1,0:T(8,128)(2,1)} %bitcast.161, bf16[320,3,512]{2,1,0:T(4,128)(2,1)} %reshape.181), kind=kOutput, calls=%fused_computation.45 | convolution fusion | flops 503316480 | bytes 3211264 | tf_op jit(solution)/shard_map/spatial_back/dot_general | solution.py:548
  117.6 39.9 %reduce_grads.1 = bf16[2,12,32,256]{3,2,1,0:T(8,128)(2,1)S(1)} custom-call(bf16[16,12,32,256]{3,2,1,0:T(8,128)(2,1)S(1)} %bitcast.120), custom_call_target="tpu_custom_call" | custom-call | tf_op jit(solution)/shard_map/reduce_grads/pallas_call | solution.py:415
  (81 shorter events, 21.0 us)
Async XLA Ops:
  53.8 1.6 copy-start
  55.4 3.5 %copy-start.3 = (bf16[12,16,32,512]{3,2,1,0:T(8,128)(2,1)S(1)}, bf16[12,16,32,512]{3,2,1,0:T(8,128)(2,1)}, u32[]{:S(2)}) copy-start(bf16[12,16,32,512]{3,2,1,0:T(8,128)(2,1)} %get-tuple-element.8) | copy-start | bytes 18874372
  61.1 7.6 %copy-start.4 = (bf16[3,16,32,512]{3,2,1,0:T(8,128)(2,1)}, bf16[3,16,32,512]{3,2,1,0:T(8,128)(2,1)S(1)}, u32[]{:S(2)}) copy-start(bf16[3,16,32,512]{3,2,1,0:T(8,128)(2,1)S(1)} %get-tuple-element.15) | copy-start | bytes 4718596
  65.3 1.3 copy-start.9
  68.7 1.3 copy-start.2
  76.3 3.1 %copy-start.1 = (bf16[4,10,16,1536]{3,2,1,0:T(8,128)(2,1)S(1)}, bf16[4,10,16,1536]{3,2,1,0:T(8,128)(2,1)}, u32[]{:S(2)}) copy-start(bf16[4,10,16,1536]{3,2,1,0:T(8,128)(2,1)} %get-tuple-element.16) | copy-start | bytes 5898244
  76.3 3.1 %copy-start.14 = (bf16[3,16,32,512]{3,2,1,0:T(8,128)(2,1)S(1)}, bf16[3,16,32,512]{3,2,1,0:T(8,128)(2,1)}, u32[]{:S(2)}) copy-start(bf16[3,16,32,512]{3,2,1,0:T(8,128)(2,1)} %get-tuple-element.13) | copy-start | bytes 4718596
  88.6 2.1 %copy-start.15 = (bf16[640,512]{1,0:T(8,128)(2,1)S(1)}, bf16[640,512]{1,0:T(8,128)(2,1)}, u32[]{:S(2)}) copy-start(bf16[640,512]{1,0:T(8,128)(2,1)} %fusion.24) | copy-start | bytes 1966084
  90.7 1.1 copy-start.10
  90.8 1.1 copy-start.17
  90.8 1.2 copy-start.18
  94.5 1.0 copy-start.7
  107.9 2.6 %copy-start.5 = (bf16[3,16,32,512]{3,2,1,0:T(8,128)(2,1)S(1)}, bf16[3,16,32,512]{3,2,1,0:T(8,128)(2,1)}, u32[]{:S(2)}) copy-start(bf16[3,16,32,512]{3,2,1,0:T(8,128)(2,1)} %copy-done.4) | copy-start | bytes 4718596
  110.5 1.3 copy-start.6
  110.5 1.4 copy-start.8
  111.3 1.7 %copy-start.20 = (bf16[512,256]{1,0:T(8,128)(2,1)S(1)}, bf16[512,256]{1,0:T(8,128)(2,1)}, u32[]{:S(2)}) copy-start(bf16[512,256]{1,0:T(8,128)(2,1)} %fusion.41) | copy-start | bytes 786436
  111.9 1.1 copy-start.19
  111.9 1.8 %copy-start.12 = (bf16[640,1536]{0,1:T(8,128)(2,1)S(1)}, bf16[640,1536]{0,1:T(8,128)(2,1)}, u32[]{:S(2)}) copy-start(bf16[640,1536]{0,1:T(8,128)(2,1)} %copy.19) | copy-start | bytes 5898244
  111.9 1.8 %copy-start.16 = (bf16[4,160,256]{2,1,0:T(8,128)(2,1)S(1)}, bf16[4,160,256]{2,1,0:T(8,128)(2,1)}, u32[]{:S(2)}) copy-start(bf16[4,160,256]{2,1,0:T(8,128)(2,1)} %constant_dynamic-slice_fusion) | copy-start | bytes 983044
  113.7 1.5 copy-start.13
  115.2 1.5 copy-start.11

commit v2 on v1

--- a/solution.py
+++ b/solution.py
@@ -439,125 +439,229 @@
     )(partial)
 
 
-def beside(frames, direction):
-    edges = ((0, 0), (1, 1), (1, 1), (0, 0))
-    wide = jnp.pad(frames, edges)
-    cols = frames.shape[2]
-    shifts = (0, 1, 2) if direction > 0 else (2, 1, 0)
-    return jnp.concatenate([wide[:, :, s : s + cols] for s in shifts], axis=-1)
+def wide_dot(left, right):
+    return jnp.dot(left, right, preferred_element_type=jnp.float32)
+
+
+def column_shifts(flat, width):
+    count = flat.shape[0]
+    column = lax.rem(lax.broadcasted_iota(jnp.int32, flat.shape, 0), width)
+    left = jnp.where(column == 0, 0.0, pltpu.roll(flat, 1, 0))
+    right = jnp.where(column == width - 1, 0.0, pltpu.roll(flat, count - 1, 0))
+    return left, flat, right
+
+
+def fill_columns(target, place, flat, width, flip):
+    channels = flat.shape[1]
+    shifts = column_shifts(flat, width)
+    for number, value in enumerate(shifts[::-1] if flip else shifts):
+        target[place : place + flat.shape[0], number * channels : (number + 1) * channels] = (
+            value.astype(jnp.bfloat16)
+        )
+
+
+def finish(tm, width, w_ref, held, upstream, s_ref, g_ref, spread, decoded_ref, input_ref):
+    channels = w_ref.shape[2]
+    own, _, pixels, _ = decoded_ref.shape
+    stride = pixels + width
+    start = tm * (own * pixels)
+    past = s_ref[pl.ds(pl.multiple_of(start, 16), own * pixels)]
+    now = s_ref[pl.ds(pl.multiple_of(start + pixels, 16), own * pixels)]
+    base = wide_dot(past, w_ref[0]) + wide_dot(now, w_ref[2])
+    ahead = base + wide_dot(past, w_ref[1])
+    behind = base + wide_dot(now, w_ref[1])
+    for frame in range(own):
+        rows = slice(frame * pixels, (frame + 1) * pixels)
+        value = held(frame).astype(jnp.float32)
+        decoded_ref[frame, 0] = (value + ahead[rows]).astype(jnp.bfloat16)
+        decoded_ref[frame, 1] = (value + behind[rows]).astype(jnp.bfloat16)
+    spread[...] = jnp.zeros_like(spread)
+    for frame in range(own):
+        place = 2 * width + (tm * own + frame) * stride
+        flat = g_ref[pl.ds(pl.multiple_of(place, 16), pixels)].astype(jnp.float32)
+        fill_columns(spread, width + frame * stride, flat, width, True)
+    span = own * stride - width
+    total = jnp.zeros((span, channels), jnp.float32)
+    for r in range(3):
+        for s in range(3):
+            total = total + contract_cols(
+                spread[(2 - r) * width : (2 - r) * width + span, s * channels : (s + 1) * channels],
+                w_ref[3 + 3 * r + s],
+            )
+    for frame in range(own):
+        part = total[frame * stride : frame * stride + pixels]
+        value = held(frame).astype(jnp.float32)
+        pair = upstream(frame).astype(jnp.float32)
+        sigmoid = 1.0 / (1.0 + jnp.exp(-value))
+        slope = sigmoid * (1.0 + value * (1.0 - sigmoid))
+        input_ref[frame] = (pair[0] + pair[1] + part * slope).astype(jnp.bfloat16)
+
+
+def compute_kernel(
+    width,
+    tm_ref,
+    w_ref,
+    u_ref,
+    c_ref,
+    p_ref,
+    decoded_ref,
+    input_ref,
+    columns,
+    columns_t,
+    s_ref,
+    s_t,
+    g_ref,
+    even_ref,
+    odd_ref,
+    spread,
+):
+    tm = tm_ref[0]
+    frames, pixels, channels = u_ref.shape
+    stride = pixels + width
+    span = frames * stride - width
+    half = p_ref.shape[3]
+    own = frames // 2
+    lanes = pl.ds(pl.multiple_of(tm * half, half), half)
+
+    def store(tap, value):
+        p_ref[:, tap] = value.astype(jnp.bfloat16).reshape(p_ref.shape[0], p_ref.shape[2], half)
+
+    for scratch in (columns, s_ref, g_ref, even_ref, odd_ref):
+        scratch[...] = jnp.zeros_like(scratch)
+    for frame in range(frames):
+        value = u_ref[frame].astype(jnp.float32)
+        fill_columns(columns, width + frame * stride, value / (1.0 + jnp.exp(-value)), width, False)
+        even_ref[(frame + 1) * pixels : (frame + 2) * pixels] = c_ref[frame, 0]
+        odd_ref[(frame + 1) * pixels : (frame + 2) * pixels] = c_ref[frame, 1]
+    columns_t[...] = columns[...].T
+
+    even = even_ref[pixels : (frames + 1) * pixels]
+    odd = odd_ref[pixels : (frames + 1) * pixels]
+    here = (
+        contract_cols(even, w_ref[2]) + contract_cols(odd, w_ref[2]) + contract_cols(odd, w_ref[1])
+    )
+    ahead = (
+        contract_cols(even, w_ref[0]) + contract_cols(odd, w_ref[0]) + contract_cols(even, w_ref[1])
+    )
+    for frame in range(frames):
+        value = here[frame * pixels : (frame + 1) * pixels]
+        if frame == 0:
+            value = value + ahead[:pixels]
+        if frame < frames - 1:
+            value = value + ahead[(frame + 1) * pixels : (frame + 2) * pixels]
+        place = 2 * width + frame * stride
+        g_ref[place : place + pixels] = value.astype(jnp.bfloat16)
+
+    depth = columns.shape[0]
+    for r in range(3):
+        begin = (2 - r) * width
+        value = wide_dot(columns_t[...], g_ref[begin : begin + depth, lanes])
+        for s in range(3):
+            store(3 + 3 * r + s, value[s * channels : (s + 1) * channels])
+
+    total = jnp.zeros((span, channels), jnp.float32)
+    for r in range(3):
+        total = total + wide_dot(
+            columns[r * width : r * width + span],
+            w_ref[3 + 3 * r : 6 + 3 * r].reshape(3 * channels, channels),
+        )
+    for frame in range(frames):
+        value = total[frame * stride : frame * stride + pixels].astype(jnp.bfloat16)
+        s_ref[(frame + 1) * pixels : (frame + 2) * pixels] = value
+        if frame == 0:
+            s_ref[:pixels] = value
+    s_t[...] = s_ref[...].T
+    extent = s_ref.shape[0]
+    past_even = wide_dot(s_t[...], even_ref[pixels : pixels + extent, lanes])
+    now_odd = wide_dot(s_t[...], odd_ref[:extent, lanes])
+    store(1, past_even + now_odd)
+    store(0, past_even + wide_dot(s_t[...], odd_ref[pixels : pixels + extent, lanes]))
+    store(2, now_odd + wide_dot(s_t[...], even_ref[:extent, lanes]))
+
+    finish(
+        tm,
+        width,
+        w_ref,
+        lambda frame: u_ref[tm * own + frame],
+        lambda frame: c_ref[tm * own + frame],
+        s_ref,
+        g_ref,
+        spread,
+        decoded_ref,
+        input_ref,
+    )
+
+
+def up_to(count, step):
+    return -(-count // step) * step
+
+
+def compute(tm, weights, clip, upstream, width, devices):
+    frames, pixels, channels = clip.shape
+    taps, half, own = weights.shape[0], channels // 2, frames // 2
+    stride = pixels + width
+    depth = up_to(width + frames * stride, 256)
+    extent = up_to((frames + 1) * pixels, 128)
+    in_vmem = pl.BlockSpec(memory_space=pltpu.VMEM)
+    kept = clip.dtype
+    return pl.pallas_call(
+        functools.partial(compute_kernel, width),
+        out_shape=(
+            jax.ShapeDtypeStruct((devices, taps, channels // devices, half), kept),
+            jax.ShapeDtypeStruct((own, 2, pixels, channels), kept),
+            jax.ShapeDtypeStruct((own, pixels, channels), kept),
+        ),
+        in_specs=[pl.BlockSpec(memory_space=pltpu.SMEM)] + [in_vmem] * 3,
+        out_specs=(in_vmem,) * 3,
+        scratch_shapes=[
+            pltpu.VMEM((depth, 3 * channels), kept),
+            pltpu.VMEM((3 * channels, depth), kept),
+            pltpu.VMEM((extent, channels), kept),
+            pltpu.VMEM((channels, extent), kept),
+            pltpu.VMEM((depth + 2 * width, channels), kept),
+            pltpu.VMEM((extent + pixels, channels), kept),
+            pltpu.VMEM((extent + pixels, channels), kept),
+            pltpu.VMEM((width + own * stride, 3 * channels), kept),
+        ],
+        compiler_params=pltpu.CompilerParams(vmem_limit_bytes=56 * 2**20),
+        cost_estimate=pl.CostEstimate(
+            flops=20 * frames * pixels * channels * channels * 2,
+            bytes_accessed=12 * 2**20,
+            transcendentals=2 * frames * pixels * channels,
+        ),
+        name="convs_and_grads",
+    )(tm, weights, clip, upstream)
 
 
 def paired_device(frames_in, cotangent, w_spatial, w_temporal):
     devices = lax.axis_size("dp")
-    tm = lax.axis_index("tm")
+    tm = lax.axis_index("tm").astype(jnp.int32).reshape(1)
     source = frames_in[0]
     own, height, width, channels = source.shape
+    frames, pixels = 2 * own, height * width
     weights, sources, upstreams = gather(
-        jnp.concatenate([w_temporal, w_spatial], axis=0), source, cotangent[0], devices
-    )
-    weights = weights.reshape(weights.shape[0], channels, channels)
-    w_t, w_s = weights[:3], weights[3:]
-    clip = sources.reshape((2 * own, height, width, channels))
-    upstream = upstreams.reshape((4 * own, height * width, channels))
-    frames = 2 * own
-    even, odd = upstream[0::2], upstream[1::2]
-    nothing = jnp.zeros_like(even[:1])
-    even_next = jnp.concatenate([even[1:], nothing], axis=0)
-    odd_next = jnp.concatenate([odd[1:], nothing], axis=0)
-
-    def back(frame_list, weight):
-        return lax.dot_general(
-            frame_list, weight, (((2,), (1,)), ((), ())), preferred_element_type=jnp.float32
-        )
-
-    with jax.named_scope("temporal_back"):
-        first = (jnp.arange(frames) == 0)[:, None, None]
-        grads = (
-            back(even, w_t[2])
-            + back(odd, w_t[2])
-            + back(odd, w_t[1])
-            + back(even_next, w_t[1])
-            + back(even_next, w_t[0])
-            + back(odd_next, w_t[0])
-        )
-        edge = (
-            back(even[:1], w_t[0]) + back(odd[:1], w_t[0]) + back(even[:1], w_t[1])
-        )
-        grads = jnp.where(first, grads + edge, grads).astype(jnp.bfloat16)
-
-    with jax.named_scope("spatial"):
-        activated = jax.nn.silu(clip.astype(jnp.float32)).astype(jnp.bfloat16)
-        columns = beside(activated, 1)
-        spatial = jnp.float32(0.0)
-        for r in range(3):
-            spatial = spatial + jnp.dot(
-                columns[:, r : r + height].reshape(-1, 3 * channels),
-                w_s[3 * r : 3 * r + 3].reshape(3 * channels, channels),
-                preferred_element_type=jnp.float32,
-            )
-        spatial = spatial.astype(jnp.bfloat16).reshape(frames, height * width, channels)
-        before = jnp.concatenate([spatial[:1], spatial[:-1]], axis=0)
-
-    with jax.named_scope("weight_grads"):
-        half = channels // 2
-        start = tm * half
-        grads_half = lax.dynamic_slice_in_dim(grads, start, half, 2).reshape(-1, half)
-        even_half = lax.dynamic_slice_in_dim(even, start, half, 2).reshape(-1, half)
-        odd_half = lax.dynamic_slice_in_dim(odd, start, half, 2).reshape(-1, half)
-        both_half = jnp.concatenate([even_half, odd_half], axis=0)
-        now, past = spatial.reshape(-1, channels), before.reshape(-1, channels)
-        parts = [
-            contract_rows(jnp.concatenate([past, past], axis=0), both_half)[None],
-            contract_rows(jnp.concatenate([past, now], axis=0), both_half)[None],
-            contract_rows(jnp.concatenate([now, now], axis=0), both_half)[None],
-        ]
-        for r in range(3):
-            window = columns[:, r : r + height].reshape(-1, 3 * channels)
-            parts.append(contract_rows(window, grads_half).reshape(3, channels, half))
-        partial = jnp.concatenate(parts, axis=0).astype(jnp.bfloat16)
-        partial = partial.reshape(12, devices, channels // devices, half).transpose(1, 0, 2, 3)
+        jnp.concatenate([w_temporal, w_spatial], axis=0),
+        source.reshape(own, pixels, channels),
+        cotangent[0].reshape(own, 2, pixels, channels),
+        devices,
+    )
+    partial, decoded, grad_input = compute(
+        tm,
+        weights.reshape(weights.shape[0], channels, channels),
+        sources.reshape(frames, pixels, channels),
+        upstreams.reshape(frames, 2, pixels, channels),
+        width,
+        devices,
+    )
     summed = reduce_grads(partial, devices)
-
-    mine = own * tm
-    with jax.named_scope("temporal"):
-        now = lax.dynamic_slice_in_dim(spatial, mine, own, 0).reshape(-1, channels)
-        past = lax.dynamic_slice_in_dim(before, mine, own, 0).reshape(-1, channels)
-        held = source.astype(jnp.float32)
-        common = (
-            jnp.dot(past, w_t[0], preferred_element_type=jnp.float32)
-            + jnp.dot(now, w_t[2], preferred_element_type=jnp.float32)
-            + held.reshape(-1, channels)
-        )
-        ahead = common + jnp.dot(past, w_t[1], preferred_element_type=jnp.float32)
-        behind = common + jnp.dot(now, w_t[1], preferred_element_type=jnp.float32)
-        decoded = jnp.stack(
-            [
-                ahead.astype(jnp.bfloat16).reshape(own, height, width, channels),
-                behind.astype(jnp.bfloat16).reshape(own, height, width, channels),
-            ],
-            axis=1,
-        ).reshape(2 * own, height, width, channels)
-    with jax.named_scope("spatial_back"):
-        mine_grads = lax.dynamic_slice_in_dim(grads, mine, own, 0).reshape(
-            own, height, width, channels
-        )
-        spread = beside(mine_grads, -1)
-        act_grad = jnp.float32(0.0)
-        for r in range(3):
-            window = spread[:, 2 - r : 2 - r + height].reshape(-1, 3, channels)
-            act_grad = act_grad + lax.dot_general(
-                window,
-                w_s[3 * r : 3 * r + 3],
-                (((1, 2), (0, 2)), ((), ())),
-                preferred_element_type=jnp.float32,
-            )
-        act_grad = act_grad.reshape(own, height, width, channels)
-        pair = cotangent[0].reshape(own, 2, height, width, channels).astype(jnp.float32)
-        grad_input = (pair[:, 0] + pair[:, 1] + act_grad * silu_slope(held)).astype(jnp.bfloat16)
-
-    inverse = 1.0 / math.sqrt(devices * 2 * frames * height * width)
+    inverse = 1.0 / math.sqrt(devices * 2 * frames * pixels)
     whole = jnp.concatenate([summed[0], summed[1]], axis=-1).astype(jnp.float32) * inverse
-    return (decoded[None], grad_input[None], whole[3:], whole[:3])
+    return (
+        decoded.reshape(1, 2 * own, height, width, channels),
+        grad_input.reshape(1, own, height, width, channels),
+        whole[3:],
+        whole[:3],
+    )
 
 
 def solution(mesh):

time: 160 us -> 117 us (0.73)
  local copies, waits for them, and re-layouts: 36.2 us -> 3.49 us
  matrix products: 25.7 us -> 0 us
  Pallas kernels: 89 us -> 111 us
  other arithmetic: 7.21 us -> 1.85 us
    dot_general x25 -> x0, matrix products: 25.7 us -> none  [the longest x3 7.43 us: paired_device(): jnp.dot(columns[:, r:r + height].reshape(-1, 3 * channels), w_s[3 * r:3 *...]
    pallas_call x0 -> x1, Pallas kernels: none -> 21.8 us  [compute(): pl.pallas_call(functools.partial(compute_kernel, width), out_shape=(jax.S...]
    reshape x6 -> x0, local copies, waits for them, and re-layouts: 16.5 us -> none  [the longest x3 10.2 us: paired_device(): columns[:, r:r + height].reshape(-1, 3 * channels)]
    slice x11 -> x2, local copies, waits for them, and re-layouts: 10.9 us -> 1.57 us  [the longest x1 0.87 us: paired_device(): whole[3:]]
    convert_element_type x3 -> x0, other arithmetic: 4.91 us -> none  [the longest x1 2.3 us: paired_device(): cotangent[0].reshape(own, 2, height, width, channels).astype(jnp.float32)]
    unnamed x45 -> x2, local copies, waits for them, and re-layouts: 6.13 us -> 1.89 us
    dynamic_slice x3 -> x0, local copies, waits for them, and re-layouts: 1.72 us -> none  [the longest x1 0.89 us: paired_device(): odd_half = lax.dynamic_slice_in_dim(odd, start, half, 2).reshape(-1, half)]
where the time goes in v2:
time: 117 us
  Pallas kernels  111 us (95%)
  local copies, waits for them, and re-layouts  3.49 us (3%)
  other arithmetic  1.85 us (2%)
    pallas_call x1, Pallas kernels, gather(): pl.pallas_call(functools.partial(gather_kernel, rows), out_shape=(jax.Sha...  49.1 us
    pallas_call x1, Pallas kernels, reduce_grads(): pl.pallas_call(functools.partial(reduce_kernel, rows), out_shape=jax.Shap...  39.9 us
    pallas_call x1, Pallas kernels, compute(): pl.pallas_call(functools.partial(compute_kernel, width), out_shape=(jax.S...  21.8 us

profile of v2, /device:TPU:0, one launch (start us, length us, event | category | flops | bytes accessed | tf_op | source)
XLA Modules:
  0.0 116.8 jit_solution(11571264885015151985)
XLA Ops:
  0.6 1.8 %pad_maximum_fusion.w_ref = bf16[12,32,512]{2,1,0:T(8,128)(2,1)} fusion(bf16[9,32,512]{2,1,0:T(8,128)(2,1)} %param.6, bf16[3,32,512]{2,1,0:T(8,128)(2,1)} %param.7), kind=kLoop, calls=%fused_computation.1 | loop fusion | flops 196608 | bytes 786432 | tf_op jit(solution)/shard_map/concatenate | solution.py:643
  2.4 49.1 %gather_weights.1 = (bf16[12,16,32,512]{3,2,1,0:T(8,128)(2,1)}, bf16[2,2,160,512]{3,2,1,0:T(8,128)(2,1)}, bf16[2,2,2,160,512]{4,3,2,1,0:T(8,128)(2,1)}) custom-call(bf16[12,32,512]{2,1,0:T(8,128)(2,1)} %pad_maximum_fusion.w_ref, bf16[2,160,512]{2,1,0:T(8,128)(2,1)} %bitcast.13, bf16[2,2,160,512]{3,2,1,0:T(8,128)(2,1)} %bitcast.12), custom_call_target="tpu_custom_call" | custom-call | tf_op jit(solution)/shard_map/gather_weights/pallas_call | solution.py:283
  51.5 21.8 %convs_and_grads.1 = (bf16[16,12,32,256]{3,2,1,0:T(8,128)(2,1)}, bf16[2,2,160,512]{3,2,1,0:T(8,128)(2,1)}, bf16[2,160,512]{2,1,0:T(8,128)(2,1)}) custom-call(s32[1]{0:T(128)} %bitcast.tm_ref, bf16[12,512,512]{2,1,0:T(8,128)(2,1)} %bitcast.14, bf16[4,160,512]{2,1,0:T(8,128)(2,1)} %bitcast.16, bf16[4,2,160,512]{3,2,1,0:T(8,128)(2,1)} %bitcast.15), custom_call_target="tpu_custom_call" | custom-call | flops 6710886400 | bytes 12582912 | tf_op jit(solution)/shard_map/convs_and_grads/pallas_call | solution.py:607
  73.3 0.0 copy-start
  73.3 1.9 %copy-done = bf16[16,12,32,256]{3,2,1,0:T(8,128)(2,1)S(1)} copy-done((bf16[16,12,32,256]{3,2,1,0:T(8,128)(2,1)S(1)}, bf16[16,12,32,256]{3,2,1,0:T(8,128)(2,1)}, u32[]{:S(2)}) %copy-start) | copy-done | bytes 3145752
  75.2 39.9 %reduce_grads.1 = bf16[2,12,32,256]{3,2,1,0:T(8,128)(2,1)S(1)} custom-call(bf16[16,12,32,256]{3,2,1,0:T(8,128)(2,1)S(1)} %copy-done), custom_call_target="tpu_custom_call" | custom-call | tf_op jit(solution)/shard_map/reduce_grads/pallas_call | solution.py:415
  115.1 0.1 convert_multiply_fusion
  115.2 0.7 slice.17
  115.9 0.9 slice.16
  (1 shorter events, 0.0 us)
Async XLA Ops:
  73.3 1.9 %copy-start = (bf16[16,12,32,256]{3,2,1,0:T(8,128)(2,1)S(1)}, bf16[16,12,32,256]{3,2,1,0:T(8,128)(2,1)}, u32[]{:S(2)}) copy-start(bf16[16,12,32,256]{3,2,1,0:T(8,128)(2,1)} %get-tuple-element.15.p_ref) | copy-start | bytes 9437188

commit v3 on v0

--- a/solution.py
+++ b/solution.py
@@ -1,9 +1,16 @@
+import functools
 import math
 
 import jax
 import jax.numpy as jnp
 from jax import lax
+from jax.experimental import pallas as pl
+from jax.experimental.pallas import tpu as pltpu
 from jax.sharding import PartitionSpec as P
+
+MESH = pl.DeviceIdType.MESH
+LINE = 4
+PARTS = 4
 
 spatial_taps = [(row_shift, col_shift) for row_shift in range(3) for col_shift in range(3)]
 
@@ -148,21 +155,503 @@
     return (decoded[None], grad_input[None], summed_s * inverse, summed_t * inverse)
 
 
+def places(line, rows):
+    index = lax.axis_index("dp")
+    core = lax.rem(index, 2)
+    row = lax.rem(index // 2, rows)
+    return index // (2 * rows), row, core, lax.axis_index("tm")
+
+
+def block_of(line, row, core, rows):
+    return (line * rows + row) * 2 + core
+
+
+def greet(peers):
+    barrier = pltpu.get_barrier_semaphore()
+    for peer in peers:
+        pl.semaphore_signal(barrier, inc=1, device_id=peer, device_id_type=MESH)
+    pl.semaphore_wait(barrier, len(peers))
+
+
+def peers_of(line, row, core, tm, rows):
+    along = [
+        (block_of(lax.rem(line + step, LINE), row, core, rows), tm) for step in range(1, LINE)
+    ]
+    across = [
+        (block_of(line, lax.rem(row + step, rows), core, rows), tm) for step in range(1, rows)
+    ]
+    sibling = (block_of(line, row, 1 - core, rows), tm)
+    partner = (block_of(line, row, core, rows), 1 - tm)
+    return along, across, sibling, partner
+
+
+def wide_dot(left, right):
+    return jnp.dot(left, right, preferred_element_type=jnp.float32)
+
+
+def column_shifts(flat, width):
+    count = flat.shape[0]
+    column = lax.rem(lax.broadcasted_iota(jnp.int32, flat.shape, 0), width)
+    left = jnp.where(column == 0, 0.0, pltpu.roll(flat, 1, 0))
+    right = jnp.where(column == width - 1, 0.0, pltpu.roll(flat, count - 1, 0))
+    return left, flat, right
+
+
+def fill_columns(target, place, flat, width, flip):
+    channels = flat.shape[1]
+    shifts = column_shifts(flat, width)
+    for number, value in enumerate(shifts[::-1] if flip else shifts):
+        target[place : place + flat.shape[0], number * channels : (number + 1) * channels] = (
+            value.astype(jnp.bfloat16)
+        )
+
+
+def up_to(count, step):
+    return -(-count // step) * step
+
+
+def section_kernel(
+    rows,
+    width,
+    w_ref,
+    u_ref,
+    c_ref,
+    decoded_ref,
+    input_ref,
+    out_ref,
+    w_all,
+    u_all,
+    c_all,
+    partial,
+    columns,
+    columns_t,
+    s_ref,
+    s_t,
+    g_ref,
+    even_ref,
+    odd_ref,
+    spread,
+    total_ref,
+    from_core,
+    to_row,
+    from_row,
+    to_line,
+    from_line,
+    send_sem,
+    recv_sem,
+    pair_send,
+    pair_recv,
+    own_sem,
+    core_send,
+    core_recv,
+    row_send,
+    row_recv,
+    line_send,
+    line_recv,
+    last_send,
+    last_recv,
+):
+    line, row, core, tm = places(LINE, rows)
+    along, across, sibling, partner = peers_of(line, row, core, tm, rows)
+    greet(along + across + [sibling, partner])
+    taps = w_ref.shape[0] // PARTS
+    me = block_of(line, row, core, rows)
+    own, _, pixels, channels = c_ref.shape
+    frames = 2 * own
+    stride = pixels + width
+    span = frames * stride - width
+    half = partial.shape[3]
+    lanes = pl.ds(pl.multiple_of(tm * half, half), half)
+    wide = jnp.float32
+    narrow = jnp.bfloat16
+    sent = []
+
+    def remote(source, target, send, recv, peer):
+        copy = pltpu.make_async_remote_copy(
+            src_ref=source,
+            dst_ref=target,
+            send_sem=send,
+            recv_sem=recv,
+            device_id=peer,
+            device_id_type=MESH,
+        )
+        copy.start()
+        return copy
+
+    def push(part, source, block, peer, slot):
+        target = w_all.at[pl.ds(part * taps, taps), block]
+        sent.append(
+            remote(source, target, send_sem.at[part, slot], recv_sem.at[part, block], peer)
+        )
+
+    def landed(part, block):
+        view = w_all.at[pl.ds(part * taps, taps), block]
+        pltpu.make_async_copy(view, view, recv_sem.at[part, block]).wait()
+        return view
+
+    first_across = LINE - 1
+    first_core = first_across + LINE * (rows - 1)
+
+    def push_own(part):
+        block = w_ref.at[pl.ds(part * taps, taps)]
+        for step, peer in enumerate(along):
+            push(part, block, me, peer, step)
+        for step, peer in enumerate(across):
+            push(part, block, me, peer, first_across + step)
+        push(part, block, me, sibling, first_core)
+
+    def relay_line(part):
+        for step in range(1, LINE):
+            block = block_of(lax.rem(line + step, LINE), row, core, rows)
+            view = landed(part, block)
+            for number, peer in enumerate(across):
+                push(part, view, block, peer, first_across + step * (rows - 1) + number)
+            push(part, view, block, sibling, first_core + step)
+
+    def relay_rows(part):
+        for number in range(1, rows):
+            for step in range(LINE):
+                block = block_of(
+                    lax.rem(line + step, LINE), lax.rem(row + number, rows), core, rows
+                )
+                push(part, landed(part, block), block, sibling, first_core + number * LINE + step)
+
+    def complete(part):
+        for number in range(rows):
+            for step in range(LINE):
+                landed(part, block_of(step, number, 1 - core, rows))
+
+    def tap(number):
+        return w_all[number].reshape(channels, channels)
+
+    order = list(range(1, LINE)) + [0]
+    core_copies, row_copies, line_copies, last_copies = {}, {}, {}, []
+    groups = ((3, 9), (0, 3))
+
+    def sum_core(group):
+        chosen = pl.ds(*groups[group])
+        for number in list(range(1, rows)) + [0]:
+            for step in order:
+                slot = number * LINE + step
+                block = block_of(
+                    lax.rem(line + step, LINE), lax.rem(row + number, rows), 1 - core, rows
+                )
+                core_copies[group, slot] = remote(
+                    partial.at[block, chosen],
+                    from_core.at[slot, chosen],
+                    core_send.at[group, slot],
+                    core_recv.at[group, slot],
+                    sibling,
+                )
+
+    def of_chip(group, number, step):
+        chosen = pl.ds(*groups[group])
+        slot = number * LINE + step
+        block = block_of(lax.rem(line + step, LINE), lax.rem(row + number, rows), core, rows)
+        core_copies[group, slot].wait_recv()
+        return partial[block, chosen].astype(wide) + from_core[slot, chosen].astype(wide)
+
+    def sum_rows(group):
+        chosen = pl.ds(*groups[group])
+        for number in range(1, rows):
+            for step in order:
+                slot = number * LINE + step
+                to_row[slot, chosen] = of_chip(group, number, step).astype(narrow)
+                row_copies[group, slot] = remote(
+                    to_row.at[slot, chosen],
+                    from_row.at[slot, chosen],
+                    row_send.at[group, slot],
+                    row_recv.at[group, slot],
+                    across[number - 1],
+                )
+
+    def of_rows(group, step):
+        value = of_chip(group, 0, step)
+        for number in range(1, rows):
+            slot = number * LINE + step
+            row_copies[group, slot].wait_recv()
+            value = value + from_row[slot, pl.ds(*groups[group])].astype(wide)
+        return value
+
+    def sum_line(group):
+        chosen = pl.ds(*groups[group])
+        for step in range(1, LINE):
+            to_line[step, chosen] = of_rows(group, step).astype(narrow)
+            line_copies[group, step] = remote(
+                to_line.at[step, chosen],
+                from_line.at[step, chosen],
+                line_send.at[group, step],
+                line_recv.at[group, step],
+                along[step - 1],
+            )
+
+    def sum_last(group):
+        chosen = pl.ds(*groups[group])
+        value = of_rows(group, 0)
+        for step in range(1, LINE):
+            line_copies[group, step].wait_recv()
+            value = value + from_line[step, chosen].astype(wide)
+        out_ref[tm, chosen] = value.astype(narrow)
+        view = out_ref.at[tm, chosen]
+        last_copies.append(
+            remote(view, view, last_send.at[group], last_recv.at[group], partner)
+        )
+
+    def store(number, value):
+        partial[:, number] = value.astype(narrow).reshape(
+            partial.shape[0], partial.shape[2], half
+        )
+
+    def lay_out():
+        for frame in range(frames):
+            value = u_all[frame // own, frame % own].astype(wide)
+            fill_columns(
+                columns, width + frame * stride, value / (1.0 + jnp.exp(-value)), width, False
+            )
+            place = slice((frame + 1) * pixels, (frame + 2) * pixels)
+            even_ref[place] = c_all[frame // own, frame % own, 0]
+            odd_ref[place] = c_all[frame // own, frame % own, 1]
+        columns_t[...] = columns[...].T
+
+    def temporal_back():
+        even = even_ref[pixels : (frames + 1) * pixels]
+        odd = odd_ref[pixels : (frames + 1) * pixels]
+        here = contract_cols(even, tap(2)) + contract_cols(odd, tap(2))
+        here = here + contract_cols(odd, tap(1))
+        ahead = contract_cols(even, tap(0)) + contract_cols(odd, tap(0))
+        ahead = ahead + contract_cols(even, tap(1))
+        for frame in range(frames):
+            value = here[frame * pixels : (frame + 1) * pixels]
+            if frame == 0:
+                value = value + ahead[:pixels]
+            if frame < frames - 1:
+                value = value + ahead[(frame + 1) * pixels : (frame + 2) * pixels]
+            place = 2 * width + frame * stride
+            g_ref[place : place + pixels] = value.astype(narrow)
+
+    def spatial_weight_grads():
+        depth = columns.shape[0]
+        for r in range(3):
+            begin = (2 - r) * width
+            value = wide_dot(columns_t[...], g_ref[begin : begin + depth, lanes])
+            for s in range(3):
+                store(3 + 3 * r + s, value[s * channels : (s + 1) * channels])
+
+    def spatial_row(r):
+        value = wide_dot(
+            columns[r * width : r * width + span],
+            w_all[3 + 3 * r : 6 + 3 * r].reshape(3 * channels, channels),
+        )
+        total_ref[...] = value if r == 0 else total_ref[...] + value
+
+    def spatial_done():
+        for frame in range(frames):
+            value = total_ref[frame * stride : frame * stride + pixels].astype(narrow)
+            s_ref[(frame + 1) * pixels : (frame + 2) * pixels] = value
+            if frame == 0:
+                s_ref[:pixels] = value
+
+    def temporal_weight_grads():
+        s_t[...] = s_ref[...].T
+        extent = s_ref.shape[0]
+        past_even = wide_dot(s_t[...], even_ref[pixels : pixels + extent, lanes])
+        now_odd = wide_dot(s_t[...], odd_ref[:extent, lanes])
+        store(1, past_even + now_odd)
+        store(0, past_even + wide_dot(s_t[...], odd_ref[pixels : pixels + extent, lanes]))
+        store(2, now_odd + wide_dot(s_t[...], even_ref[:extent, lanes]))
+
+    def decode():
+        start = tm * (own * pixels)
+        past = s_ref[pl.ds(pl.multiple_of(start, 16), own * pixels)]
+        now = s_ref[pl.ds(pl.multiple_of(start + pixels, 16), own * pixels)]
+        base = wide_dot(past, tap(0)) + wide_dot(now, tap(2))
+        first = base + wide_dot(past, tap(1))
+        second = base + wide_dot(now, tap(1))
+        for frame in range(own):
+            place = slice(frame * pixels, (frame + 1) * pixels)
+            value = u_all[tm, frame].astype(wide)
+            decoded_ref[frame, 0] = (value + first[place]).astype(narrow)
+            decoded_ref[frame, 1] = (value + second[place]).astype(narrow)
+
+    def spatial_back():
+        for frame in range(own):
+            place = 2 * width + (tm * own + frame) * stride
+            flat = g_ref[pl.ds(pl.multiple_of(place, 16), pixels)].astype(wide)
+            fill_columns(spread, width + frame * stride, flat, width, True)
+        count = own * stride - width
+        value = jnp.zeros((count, channels), wide)
+        for r in range(3):
+            begin = (2 - r) * width
+            for s in range(3):
+                value = value + contract_cols(
+                    spread[begin : begin + count, s * channels : (s + 1) * channels],
+                    tap(3 + 3 * r + s),
+                )
+        for frame in range(own):
+            part = value[frame * stride : frame * stride + pixels]
+            held = u_all[tm, frame].astype(wide)
+            sigmoid = 1.0 / (1.0 + jnp.exp(-held))
+            slope = sigmoid * (1.0 + held * (1.0 - sigmoid))
+            pair = c_all[tm, frame, 0].astype(wide) + c_all[tm, frame, 1].astype(wide)
+            input_ref[frame] = (pair + part * slope).astype(narrow)
+
+    push_own(0)
+    pairs = [
+        remote(u_ref, u_all.at[tm], pair_send.at[0], pair_recv.at[0], partner),
+        remote(c_ref, c_all.at[tm], pair_send.at[1], pair_recv.at[1], partner),
+    ]
+    for part in range(1, PARTS):
+        push_own(part)
+    kept = [
+        pltpu.make_async_copy(w_ref, w_all.at[:, me], own_sem.at[0]),
+        pltpu.make_async_copy(u_ref, u_all.at[tm], own_sem.at[1]),
+        pltpu.make_async_copy(c_ref, c_all.at[tm], own_sem.at[2]),
+    ]
+    for copy in kept:
+        copy.start()
+    for scratch in (columns, s_ref, g_ref, even_ref, odd_ref, spread):
+        scratch[...] = jnp.zeros_like(scratch)
+    relay_line(0)
+    relay_line(1)
+    relay_rows(0)
+    for copy in kept:
+        copy.wait()
+    for copy in pairs:
+        copy.wait_recv()
+    lay_out()
+    relay_line(2)
+    relay_rows(1)
+    complete(0)
+    temporal_back()
+    relay_line(3)
+    relay_rows(2)
+    spatial_weight_grads()
+    sum_core(0)
+    complete(1)
+    spatial_row(0)
+    relay_rows(3)
+    sum_rows(0)
+    complete(2)
+    spatial_row(1)
+    complete(3)
+    spatial_row(2)
+    spatial_done()
+    temporal_weight_grads()
+    sum_core(1)
+    sum_line(0)
+    sum_rows(1)
+    decode()
+    sum_line(1)
+    spatial_back()
+    sum_last(0)
+    sum_last(1)
+    for copy in sent + pairs:
+        copy.wait_send()
+    for copies in (core_copies, row_copies, line_copies):
+        for copy in copies.values():
+            copy.wait_send()
+    for copy in last_copies:
+        copy.wait()
+
+
+def section(weights, source, upstream, width, devices):
+    rows = devices // (2 * LINE)
+    own, pixels, channels = source.shape
+    taps, block, _ = weights.shape
+    frames, half = 2 * own, channels // 2
+    stride = pixels + width
+    depth = up_to(width + frames * stride, 256)
+    extent = up_to((frames + 1) * pixels, 128)
+    many = rows * LINE
+    slots = (LINE - 1) + LINE * (rows - 1) + many
+    kept = source.dtype
+    anywhere = pl.BlockSpec(memory_space=pl.ANY)
+    in_vmem = pl.BlockSpec(memory_space=pltpu.VMEM)
+    dma = pltpu.SemaphoreType.DMA
+    return pl.pallas_call(
+        functools.partial(section_kernel, rows, width),
+        out_shape=(
+            jax.ShapeDtypeStruct((own, 2, pixels, channels), kept),
+            jax.ShapeDtypeStruct((own, pixels, channels), kept),
+            jax.ShapeDtypeStruct((2, taps, block, half), kept),
+        ),
+        in_specs=[anywhere] * 3,
+        out_specs=(in_vmem,) * 3,
+        scratch_shapes=[
+            pltpu.VMEM((taps, devices, block, channels), kept),
+            pltpu.VMEM((2, own, pixels, channels), kept),
+            pltpu.VMEM((2, own, 2, pixels, channels), kept),
+            pltpu.VMEM((devices, taps, block, half), kept),
+            pltpu.VMEM((depth, 3 * channels), kept),
+            pltpu.VMEM((3 * channels, depth), kept),
+            pltpu.VMEM((extent, channels), kept),
+            pltpu.VMEM((channels, extent), kept),
+            pltpu.VMEM((depth + 2 * width, channels), kept),
+            pltpu.VMEM((extent + pixels, channels), kept),
+            pltpu.VMEM((extent + pixels, channels), kept),
+            pltpu.VMEM((width + own * stride, 3 * channels), kept),
+            pltpu.VMEM((frames * stride - width, channels), jnp.float32),
+            pltpu.VMEM((many, taps, block, half), kept),
+            pltpu.VMEM((many, taps, block, half), kept),
+            pltpu.VMEM((many, taps, block, half), kept),
+            pltpu.VMEM((LINE, taps, block, half), kept),
+            pltpu.VMEM((LINE, taps, block, half), kept),
+            dma((PARTS, slots)),
+            dma((PARTS, devices)),
+            dma((2,)),
+            dma((2,)),
+            dma((3,)),
+            dma((2, many)),
+            dma((2, many)),
+            dma((2, many)),
+            dma((2, many)),
+            dma((2, LINE)),
+            dma((2, LINE)),
+            dma((2,)),
+            dma((2,)),
+        ],
+        compiler_params=pltpu.CompilerParams(
+            collective_id=0, has_side_effects=True, vmem_limit_bytes=58 * 2**20
+        ),
+        cost_estimate=pl.CostEstimate(
+            flops=20 * frames * pixels * channels * channels * 2,
+            bytes_accessed=12 * 2**20,
+            transcendentals=2 * frames * pixels * channels,
+        ),
+        name="section",
+    )(weights, source, upstream)
+
+
+def paired_device(frames_in, cotangent, w_spatial, w_temporal):
+    devices = lax.axis_size("dp")
+    source = frames_in[0]
+    own, height, width, channels = source.shape
+    frames, pixels = 2 * own, height * width
+    decoded, grad_input, summed = section(
+        jnp.concatenate([w_temporal, w_spatial], axis=0),
+        source.reshape(own, pixels, channels),
+        cotangent[0].reshape(own, 2, pixels, channels),
+        width,
+        devices,
+    )
+    inverse = 1.0 / math.sqrt(devices * 2 * frames * pixels)
+    whole = jnp.concatenate([summed[0], summed[1]], axis=-1).astype(jnp.float32) * inverse
+    return (
+        decoded.reshape(1, 2 * own, height, width, channels),
+        grad_input.reshape(1, own, height, width, channels),
+        whole[3:],
+        whole[:3],
+    )
+
+
 def solution(mesh):
+    clip_split = P("dp", "tm", None, None, None)
+    rows_split = P(None, "dp", None)
+    paired = mesh.shape["tm"] == 2 and mesh.shape["dp"] % (2 * LINE) == 0
     return jax.shard_map(
-        per_device,
+        paired_device if paired else per_device,
         mesh=mesh,
-        in_specs=(
-            P("dp", "tm", None, None, None),
-            P("dp", "tm", None, None, None),
-            P(None, "dp", None),
-            P(None, "dp", None),
-        ),
-        out_specs=(
-            P("dp", "tm", None, None, None),
-            P("dp", "tm", None, None, None),
-            P(None, "dp", None),
-            P(None, "dp", None),
-        ),
+        in_specs=(clip_split, clip_split, rows_split, rows_split),
+        out_specs=(clip_split, clip_split, rows_split, rows_split),
         check_vma=False,
     )

time: 362 us -> 87.5 us (0.24)
  the two profiles are of different devices: /device:TPU:0 before, /device:TPU:24 now
where the time goes in v3:
time: 87.5 us; the launch traced here: 87.2 us
  Pallas kernels  79.8 us (91%)
  local copies, waits for them, and re-layouts  4.93 us (6%)
  other arithmetic  1.85 us (2%)
    pallas_call x1, Pallas kernels, section(): pl.pallas_call(functools.partial(section_kernel, rows, width), out_shape=...  79.8 us
    unnamed x6, local copies, waits for them, and re-layouts  2.31 us
    concatenate x1, other arithmetic, paired_device(): jnp.concatenate([w_temporal, w_spatial], axis=0)  1.76 us

profile of v3, /device:TPU:24, one launch (start us, length us, event | category | flops | bytes accessed | tf_op | source)
XLA Modules:
  0.0 87.2 jit_solution(11022304736238567318)
XLA Ops:
  0.6 1.8 %pad_maximum_fusion.w_ref = bf16[12,32,512]{2,1,0:T(8,128)(2,1)} fusion(bf16[9,32,512]{2,1,0:T(8,128)(2,1)} %param.6, bf16[3,32,512]{2,1,0:T(8,128)(2,1)} %param.7), kind=kLoop, calls=%fused_computation.1 | loop fusion | flops 196608 | bytes 786432 | tf_op jit(solution)/shard_map/concatenate | solution.py:631
  2.4 79.8 %section.1 = (bf16[2,2,160,512]{3,2,1,0:T(8,128)(2,1)}, bf16[2,160,512]{2,1,0:T(8,128)(2,1)}, bf16[2,12,32,256]{3,2,1,0:T(8,128)(2,1)}) custom-call(bf16[12,32,512]{2,1,0:T(8,128)(2,1)} %pad_maximum_fusion.w_ref, bf16[2,160,512]{2,1,0:T(8,128)(2,1)} %bitcast.11, bf16[2,2,160,512]{3,2,1,0:T(8,128)(2,1)} %bitcast.10), custom_call_target="tpu_custom_call" | custom-call | flops 6710886400 | bytes 12582912 | tf_op jit(solution)/shard_map/section/pallas_call | solution.py:571
  82.2 1.0 %slice_bitcast_fusion.1 = (bf16[12,32,256]{2,1,0:T(8,128)(2,1)S(1)}, bf16[12,32,256]{2,1,0:T(8,128)(2,1)S(1)}) fusion(bf16[2,12,32,256]{3,2,1,0:T(8,128)(2,1)} %get-tuple-element.9), kind=kLoop, calls=%fused_computation.3 | loop fusion | bytes 786432 | tf_op jit(solution)/shard_map/squeeze | solution.py:638
  83.2 0.1 convert_multiply_fusion
  83.3 0.7 slice.17
  84.0 0.0 copy-start
  84.0 0.9 slice.16
  84.9 0.4 copy-done
  85.3 0.0 copy-start.1
  85.3 0.8 copy.10
  86.2 0.3 copy-done.1
  86.5 0.7 copy.11
Async XLA Ops:
  84.0 1.3 %copy-start = (bf16[2,2,160,512]{3,2,1,0:T(8,128)(2,1)S(1)}, bf16[2,2,160,512]{3,2,1,0:T(8,128)(2,1)}, u32[]{:S(2)}) copy-start(bf16[2,2,160,512]{3,2,1,0:T(8,128)(2,1)} %get-tuple-element.7) | copy-start | bytes 1966084
  85.3 1.2 %copy-start.1 = (bf16[2,160,512]{2,1,0:T(8,128)(2,1)S(1)}, bf16[2,160,512]{2,1,0:T(8,128)(2,1)}, u32[]{:S(2)}) copy-start(bf16[2,160,512]{2,1,0:T(8,128)(2,1)} %get-tuple-element.8) | copy-start | bytes 983044

commit v4 on v3

--- a/solution.py
+++ b/solution.py
@@ -213,13 +213,17 @@
 def section_kernel(
     rows,
     width,
-    w_ref,
+    wt_ref,
+    ws_ref,
     u_ref,
     c_ref,
     decoded_ref,
     input_ref,
+    gs_ref,
+    gt_ref,
     out_ref,
-    w_all,
+    wt_all,
+    ws_all,
     u_all,
     c_all,
     partial,
@@ -232,6 +236,10 @@
     odd_ref,
     spread,
     total_ref,
+    s_halves,
+    act_total,
+    act_out,
+    act_in,
     from_core,
     to_row,
     from_row,
@@ -254,7 +262,7 @@
     line, row, core, tm = places(LINE, rows)
     along, across, sibling, partner = peers_of(line, row, core, tm, rows)
     greet(along + across + [sibling, partner])
-    taps = w_ref.shape[0] // PARTS
+    taps = wt_ref.shape[0]
     me = block_of(line, row, core, rows)
     own, _, pixels, channels = c_ref.shape
     frames = 2 * own
@@ -278,14 +286,18 @@
         copy.start()
         return copy
 
+    def place_of(part, block):
+        if part == 0:
+            return wt_all.at[:, block]
+        return ws_all.at[pl.ds((part - 1) * taps, taps), block]
+
     def push(part, source, block, peer, slot):
-        target = w_all.at[pl.ds(part * taps, taps), block]
         sent.append(
-            remote(source, target, send_sem.at[part, slot], recv_sem.at[part, block], peer)
+            remote(source, place_of(part, block), send_sem.at[part, slot], recv_sem.at[part, block], peer)
         )
 
     def landed(part, block):
-        view = w_all.at[pl.ds(part * taps, taps), block]
+        view = place_of(part, block)
         pltpu.make_async_copy(view, view, recv_sem.at[part, block]).wait()
         return view
 
@@ -293,7 +305,7 @@
     first_core = first_across + LINE * (rows - 1)
 
     def push_own(part):
-        block = w_ref.at[pl.ds(part * taps, taps)]
+        block = wt_ref if part == 0 else ws_ref.at[pl.ds((part - 1) * taps, taps), :, lanes]
         for step, peer in enumerate(along):
             push(part, block, me, peer, step)
         for step, peer in enumerate(across):
@@ -322,7 +334,7 @@
                 landed(part, block_of(step, number, 1 - core, rows))
 
     def tap(number):
-        return w_all[number].reshape(channels, channels)
+        return wt_all[number].reshape(channels, channels)
 
     order = list(range(1, LINE)) + [0]
     core_copies, row_copies, line_copies, last_copies = {}, {}, {}, []
@@ -440,16 +452,23 @@
     def spatial_row(r):
         value = wide_dot(
             columns[r * width : r * width + span],
-            w_all[3 + 3 * r : 6 + 3 * r].reshape(3 * channels, channels),
+            ws_all[3 * r : 3 * r + 3].reshape(3 * channels, half),
         )
         total_ref[...] = value if r == 0 else total_ref[...] + value
 
     def spatial_done():
         for frame in range(frames):
             value = total_ref[frame * stride : frame * stride + pixels].astype(narrow)
-            s_ref[(frame + 1) * pixels : (frame + 2) * pixels] = value
-            if frame == 0:
-                s_ref[:pixels] = value
+            s_halves[tm, frame * pixels : (frame + 1) * pixels] = value
+        view = s_halves.at[tm]
+        pairs.append(remote(view, view, pair_send.at[2], pair_recv.at[2], partner))
+
+    def spatial_join():
+        pairs[2].wait_recv()
+        for side in range(2):
+            columns_of = slice(side * half, (side + 1) * half)
+            s_ref[pixels : (frames + 1) * pixels, columns_of] = s_halves[side]
+            s_ref[:pixels, columns_of] = s_halves[side, :pixels]
 
     def temporal_weight_grads():
         s_t[...] = s_ref[...].T
@@ -473,22 +492,31 @@
             decoded_ref[frame, 0] = (value + first[place]).astype(narrow)
             decoded_ref[frame, 1] = (value + second[place]).astype(narrow)
 
+    def rows_of(side, frame):
+        return pl.ds(pl.multiple_of((side * own + frame) * stride, 16), pixels)
+
     def spatial_back():
-        for frame in range(own):
-            place = 2 * width + (tm * own + frame) * stride
-            flat = g_ref[pl.ds(pl.multiple_of(place, 16), pixels)].astype(wide)
+        for frame in range(frames):
+            place = 2 * width + frame * stride
+            flat = g_ref[place : place + pixels, lanes].astype(wide)
             fill_columns(spread, width + frame * stride, flat, width, True)
-        count = own * stride - width
-        value = jnp.zeros((count, channels), wide)
+        value = jnp.zeros((span, channels), wide)
         for r in range(3):
             begin = (2 - r) * width
             for s in range(3):
                 value = value + contract_cols(
-                    spread[begin : begin + count, s * channels : (s + 1) * channels],
-                    tap(3 + 3 * r + s),
+                    spread[begin : begin + span, s * half : (s + 1) * half],
+                    ws_all[3 * r + s].reshape(channels, half),
                 )
+        act_total[...] = value
         for frame in range(own):
-            part = value[frame * stride : frame * stride + pixels]
+            act_out[frame] = act_total[rows_of(1 - tm, frame)].astype(narrow)
+        pairs.append(remote(act_out, act_in, pair_send.at[3], pair_recv.at[3], partner))
+
+    def input_grads():
+        pairs[3].wait_recv()
+        for frame in range(own):
+            part = act_total[rows_of(tm, frame)] + act_in[frame].astype(wide)
             held = u_all[tm, frame].astype(wide)
             sigmoid = 1.0 / (1.0 + jnp.exp(-held))
             slope = sigmoid * (1.0 + held * (1.0 - sigmoid))
@@ -503,7 +531,8 @@
     for part in range(1, PARTS):
         push_own(part)
     kept = [
-        pltpu.make_async_copy(w_ref, w_all.at[:, me], own_sem.at[0]),
+        pltpu.make_async_copy(wt_ref, wt_all.at[:, me], own_sem.at[0]),
+        pltpu.make_async_copy(ws_ref.at[:, :, lanes], ws_all.at[:, me], own_sem.at[3]),
         pltpu.make_async_copy(u_ref, u_all.at[tm], own_sem.at[1]),
         pltpu.make_async_copy(c_ref, c_all.at[tm], own_sem.at[2]),
     ]
@@ -536,13 +565,15 @@
     complete(3)
     spatial_row(2)
     spatial_done()
+    spatial_back()
+    sum_line(0)
+    spatial_join()
     temporal_weight_grads()
     sum_core(1)
-    sum_line(0)
     sum_rows(1)
     decode()
     sum_line(1)
-    spatial_back()
+    input_grads()
     sum_last(0)
     sum_last(1)
     for copy in sent + pairs:
@@ -552,12 +583,16 @@
             copy.wait_send()
     for copy in last_copies:
         copy.wait()
-
-
-def section(weights, source, upstream, width, devices):
+    for side in range(2):
+        gt_ref[:, :, side * half : (side + 1) * half] = out_ref[side, :taps]
+        gs_ref[:, :, side * half : (side + 1) * half] = out_ref[side, taps:]
+
+
+def section(w_temporal, w_spatial, source, upstream, width, devices):
     rows = devices // (2 * LINE)
     own, pixels, channels = source.shape
-    taps, block, _ = weights.shape
+    block = w_temporal.shape[1]
+    taps = w_temporal.shape[0] + w_spatial.shape[0]
     frames, half = 2 * own, channels // 2
     stride = pixels + width
     depth = up_to(width + frames * stride, 256)
@@ -573,12 +608,15 @@
         out_shape=(
             jax.ShapeDtypeStruct((own, 2, pixels, channels), kept),
             jax.ShapeDtypeStruct((own, pixels, channels), kept),
-            jax.ShapeDtypeStruct((2, taps, block, half), kept),
+            jax.ShapeDtypeStruct(w_spatial.shape, kept),
+            jax.ShapeDtypeStruct(w_temporal.shape, kept),
         ),
-        in_specs=[anywhere] * 3,
-        out_specs=(in_vmem,) * 3,
+        in_specs=[anywhere] * 4,
+        out_specs=(in_vmem,) * 4,
         scratch_shapes=[
-            pltpu.VMEM((taps, devices, block, channels), kept),
+            pltpu.VMEM((2, taps, block, half), kept),
+            pltpu.VMEM((w_temporal.shape[0], devices, block, channels), kept),
+            pltpu.VMEM((w_spatial.shape[0], devices, block, half), kept),
             pltpu.VMEM((2, own, pixels, channels), kept),
             pltpu.VMEM((2, own, 2, pixels, channels), kept),
             pltpu.VMEM((devices, taps, block, half), kept),
@@ -589,8 +627,12 @@
             pltpu.VMEM((depth + 2 * width, channels), kept),
             pltpu.VMEM((extent + pixels, channels), kept),
             pltpu.VMEM((extent + pixels, channels), kept),
-            pltpu.VMEM((width + own * stride, 3 * channels), kept),
+            pltpu.VMEM((width + frames * stride, 3 * half), kept),
+            pltpu.VMEM((frames * stride - width, half), jnp.float32),
+            pltpu.VMEM((2, frames * pixels, half), kept),
             pltpu.VMEM((frames * stride - width, channels), jnp.float32),
+            pltpu.VMEM((own, pixels, channels), kept),
+            pltpu.VMEM((own, pixels, channels), kept),
             pltpu.VMEM((many, taps, block, half), kept),
             pltpu.VMEM((many, taps, block, half), kept),
             pltpu.VMEM((many, taps, block, half), kept),
@@ -598,9 +640,9 @@
             pltpu.VMEM((LINE, taps, block, half), kept),
             dma((PARTS, slots)),
             dma((PARTS, devices)),
-            dma((2,)),
-            dma((2,)),
-            dma((3,)),
+            dma((4,)),
+            dma((4,)),
+            dma((4,)),
             dma((2, many)),
             dma((2, many)),
             dma((2, many)),
@@ -619,7 +661,7 @@
             transcendentals=2 * frames * pixels * channels,
         ),
         name="section",
-    )(weights, source, upstream)
+    )(w_temporal, w_spatial, source, upstream)
 
 
 def paired_device(frames_in, cotangent, w_spatial, w_temporal):
@@ -627,20 +669,20 @@
     source = frames_in[0]
     own, height, width, channels = source.shape
     frames, pixels = 2 * own, height * width
-    decoded, grad_input, summed = section(
-        jnp.concatenate([w_temporal, w_spatial], axis=0),
+    decoded, grad_input, grad_s, grad_t = section(
+        w_temporal,
+        w_spatial,
         source.reshape(own, pixels, channels),
         cotangent[0].reshape(own, 2, pixels, channels),
         width,
         devices,
     )
     inverse = 1.0 / math.sqrt(devices * 2 * frames * pixels)
-    whole = jnp.concatenate([summed[0], summed[1]], axis=-1).astype(jnp.float32) * inverse
     return (
         decoded.reshape(1, 2 * own, height, width, channels),
         grad_input.reshape(1, own, height, width, channels),
-        whole[3:],
-        whole[:3],
+        grad_s.astype(jnp.float32) * inverse,
+        grad_t.astype(jnp.float32) * inverse,
     )
 
 

time: 87.5 us -> 74.9 us (0.86)
  the two profiles are of different devices: /device:TPU:24 before, /device:TPU:0 now
where the time goes in v4:
time: 74.9 us; the launch traced here: 74.7 us
  Pallas kernels  69.5 us (93%)
  other arithmetic  2.64 us (4%)
  local copies, waits for them, and re-layouts  1.89 us (3%)
    pallas_call x1, Pallas kernels, section(): pl.pallas_call(functools.partial(section_kernel, rows, width), out_shape=...  69.5 us
    mul x1, other arithmetic, paired_device(): grad_s.astype(jnp.float32) * inverse  1.94 us
    unnamed x8, local copies, waits for them, and re-layouts  1.89 us

profile of v4, /device:TPU:0, one launch (start us, length us, event | category | flops | bytes accessed | tf_op | source)
XLA Modules:
  0.0 74.7 jit_solution(17258217339997542066)
XLA Ops:
  0.6 69.5 %section.1 = (bf16[2,2,160,512]{3,2,1,0:T(8,128)(2,1)}, bf16[2,160,512]{2,1,0:T(8,128)(2,1)}, bf16[9,32,512]{2,1,0:T(8,128)(2,1)}, bf16[3,32,512]{2,1,0:T(8,128)(2,1)}) custom-call(bf16[3,32,512]{2,1,0:T(8,128)(2,1)} %wt_ref.1, bf16[9,32,512]{2,1,0:T(8,128)(2,1)} %ws_ref.1, bf16[2,160,512]{2,1,0:T(8,128)(2,1)} %bitcast.7, bf16[2,2,160,512]{3,2,1,0:T(8,128)(2,1)} %bitcast.6), custom_call_target="tpu_custom_call" | custom-call | flops 6710886400 | bytes 12582912 | tf_op jit(solution)/shard_map/section/pallas_call | solution.py:606
  70.1 0.0 copy-start
  70.1 0.0 copy-start.2
  70.2 1.9 %convert_multiply_fusion = f32[9,32,512]{2,1,0:T(8,128)} fusion(bf16[9,32,512]{2,1,0:T(8,128)(2,1)} %get-tuple-element.10), kind=kLoop, calls=%fused_computation | loop fusion | flops 294912 | bytes 884736 | tf_op jit(solution)/shard_map/mul | solution.py:684
  72.1 0.0 copy-done.2
  72.1 0.7 convert_multiply_fusion.1
  72.8 0.0 copy-done
  72.8 0.0 copy-start.1
  72.8 0.8 %copy.10 = bf16[1,4,10,16,512]{4,3,2,1,0:T(8,128)(2,1)} copy(bf16[1,4,10,16,512]{4,3,2,1,0:T(8,128)(2,1)S(1)} %bitcast.4) | data formatting | bytes 1310720
  73.6 0.3 copy-done.1
  74.0 0.7 copy.11
Async XLA Ops:
  70.1 2.7 %copy-start = (bf16[2,2,160,512]{3,2,1,0:T(8,128)(2,1)S(1)}, bf16[2,2,160,512]{3,2,1,0:T(8,128)(2,1)}, u32[]{:S(2)}) copy-start(bf16[2,2,160,512]{3,2,1,0:T(8,128)(2,1)} %get-tuple-element.8) | copy-start | bytes 1966084
  70.1 2.0 %copy-start.2 = (bf16[3,32,512]{2,1,0:T(8,128)(2,1)S(1)}, bf16[3,32,512]{2,1,0:T(8,128)(2,1)}, u32[]{:S(2)}) copy-start(bf16[3,32,512]{2,1,0:T(8,128)(2,1)} %get-tuple-element.11) | copy-start | bytes 294916
  72.8 1.2 %copy-start.1 = (bf16[2,160,512]{2,1,0:T(8,128)(2,1)S(1)}, bf16[2,160,512]{2,1,0:T(8,128)(2,1)}, u32[]{:S(2)}) copy-start(bf16[2,160,512]{2,1,0:T(8,128)(2,1)} %get-tuple-element.9) | copy-start | bytes 983044

commit v5 on v4

--- a/solution.py
+++ b/solution.py
@@ -213,6 +213,7 @@
 def section_kernel(
     rows,
     width,
+    inverse,
     wt_ref,
     ws_ref,
     u_ref,
@@ -385,9 +386,9 @@
             value = value + from_row[slot, pl.ds(*groups[group])].astype(wide)
         return value
 
-    def sum_line(group):
+    def sum_line(group, steps):
         chosen = pl.ds(*groups[group])
-        for step in range(1, LINE):
+        for step in steps:
             to_line[step, chosen] = of_rows(group, step).astype(narrow)
             line_copies[group, step] = remote(
                 to_line.at[step, chosen],
@@ -420,10 +421,13 @@
             fill_columns(
                 columns, width + frame * stride, value / (1.0 + jnp.exp(-value)), width, False
             )
+        columns_t[...] = columns[...].T
+
+    def lay_out_grads():
+        for frame in range(frames):
             place = slice((frame + 1) * pixels, (frame + 2) * pixels)
             even_ref[place] = c_all[frame // own, frame % own, 0]
             odd_ref[place] = c_all[frame // own, frame % own, 1]
-        columns_t[...] = columns[...].T
 
     def temporal_back():
         even = even_ref[pixels : (frames + 1) * pixels]
@@ -543,22 +547,23 @@
     relay_line(0)
     relay_line(1)
     relay_rows(0)
+    relay_line(2)
+    relay_rows(1)
     for copy in kept:
         copy.wait()
-    for copy in pairs:
-        copy.wait_recv()
+    pairs[0].wait_recv()
     lay_out()
-    relay_line(2)
-    relay_rows(1)
+    relay_line(3)
+    relay_rows(2)
+    pairs[1].wait_recv()
+    lay_out_grads()
     complete(0)
     temporal_back()
-    relay_line(3)
-    relay_rows(2)
+    relay_rows(3)
     spatial_weight_grads()
     sum_core(0)
     complete(1)
     spatial_row(0)
-    relay_rows(3)
     sum_rows(0)
     complete(2)
     spatial_row(1)
@@ -566,13 +571,14 @@
     spatial_row(2)
     spatial_done()
     spatial_back()
-    sum_line(0)
+    sum_line(0, range(1, LINE - 1))
     spatial_join()
     temporal_weight_grads()
     sum_core(1)
+    sum_line(0, range(LINE - 1, LINE))
     sum_rows(1)
     decode()
-    sum_line(1)
+    sum_line(1, range(1, LINE))
     input_grads()
     sum_last(0)
     sum_last(1)
@@ -584,8 +590,9 @@
     for copy in last_copies:
         copy.wait()
     for side in range(2):
-        gt_ref[:, :, side * half : (side + 1) * half] = out_ref[side, :taps]
-        gs_ref[:, :, side * half : (side + 1) * half] = out_ref[side, taps:]
+        place = slice(side * half, (side + 1) * half)
+        gt_ref[:, :, place] = out_ref[side, :taps].astype(wide) * inverse
+        gs_ref[:, :, place] = out_ref[side, taps:].astype(wide) * inverse
 
 
 def section(w_temporal, w_spatial, source, upstream, width, devices):
@@ -597,6 +604,7 @@
     stride = pixels + width
     depth = up_to(width + frames * stride, 256)
     extent = up_to((frames + 1) * pixels, 128)
+    inverse = 1.0 / math.sqrt(devices * 2 * frames * pixels)
     many = rows * LINE
     slots = (LINE - 1) + LINE * (rows - 1) + many
     kept = source.dtype
@@ -604,12 +612,12 @@
     in_vmem = pl.BlockSpec(memory_space=pltpu.VMEM)
     dma = pltpu.SemaphoreType.DMA
     return pl.pallas_call(
-        functools.partial(section_kernel, rows, width),
+        functools.partial(section_kernel, rows, width, inverse),
         out_shape=(
             jax.ShapeDtypeStruct((own, 2, pixels, channels), kept),
             jax.ShapeDtypeStruct((own, pixels, channels), kept),
-            jax.ShapeDtypeStruct(w_spatial.shape, kept),
-            jax.ShapeDtypeStruct(w_temporal.shape, kept),
+            jax.ShapeDtypeStruct(w_spatial.shape, jnp.float32),
+            jax.ShapeDtypeStruct(w_temporal.shape, jnp.float32),
         ),
         in_specs=[anywhere] * 4,
         out_specs=(in_vmem,) * 4,
@@ -668,7 +676,7 @@
     devices = lax.axis_size("dp")
     source = frames_in[0]
     own, height, width, channels = source.shape
-    frames, pixels = 2 * own, height * width
+    pixels = height * width
     decoded, grad_input, grad_s, grad_t = section(
         w_temporal,
         w_spatial,
@@ -677,12 +685,11 @@
         width,
         devices,
     )
-    inverse = 1.0 / math.sqrt(devices * 2 * frames * pixels)
     return (
         decoded.reshape(1, 2 * own, height, width, channels),
         grad_input.reshape(1, own, height, width, channels),
-        grad_s.astype(jnp.float32) * inverse,
-        grad_t.astype(jnp.float32) * inverse,
+        grad_s,
+        grad_t,
     )
 
 

time: 74.9 us -> 77.2 us (1.031)
  local copies, waits for them, and re-layouts: 1.89 us -> 4.99 us
  other arithmetic: 2.64 us -> 0 us
  Pallas kernels: 69.5 us -> 71.3 us
    unnamed x8 -> x10, local copies, waits for them, and re-layouts: 1.89 us -> 4.99 us
    mul x2 -> x0, other arithmetic: 2.64 us -> none  [the longest x1 1.94 us: paired_device(): grad_s.astype(jnp.float32) * inverse]
    pallas_call x1, Pallas kernels: 69.5 us -> 71.3 us  [section(): pl.pallas_call(functools.partial(section_kernel, rows, width, inverse), o...]
where the time goes in v5:
time: 77.2 us; the launch traced here: 77 us
  Pallas kernels  71.3 us (92%)
  local copies, waits for them, and re-layouts  4.99 us (6%)
    pallas_call x1, Pallas kernels, section(): pl.pallas_call(functools.partial(section_kernel, rows, width, inverse), o...  71.3 us
    unnamed x10, local copies, waits for them, and re-layouts  4.99 us

profile of v5, /device:TPU:0, one launch (start us, length us, event | category | flops | bytes accessed | tf_op | source)
XLA Modules:
  0.0 77.0 jit_solution(1960709178590352071)
XLA Ops:
  0.6 71.3 %section.1 = (bf16[2,2,160,512]{3,2,1,0:T(8,128)(2,1)}, bf16[2,160,512]{2,1,0:T(8,128)(2,1)}, f32[9,32,512]{2,1,0:T(8,128)}, f32[3,32,512]{2,1,0:T(8,128)}) custom-call(bf16[3,32,512]{2,1,0:T(8,128)(2,1)} %wt_ref.1, bf16[9,32,512]{2,1,0:T(8,128)(2,1)} %ws_ref.1, bf16[2,160,512]{2,1,0:T(8,128)(2,1)} %bitcast.7, bf16[2,2,160,512]{3,2,1,0:T(8,128)(2,1)} %bitcast.6), custom_call_target="tpu_custom_call" | custom-call | flops 6710886400 | bytes 12582912 | tf_op jit(solution)/shard_map/section/pallas_call | solution.py:614
  72.0 0.0 copy-start.1
  72.0 2.0 %copy.12 = bf16[1,4,10,16,512]{4,3,2,1,0:T(8,128)(2,1)} copy(bf16[1,4,10,16,512]{4,3,2,1,0:T(8,128)(2,1)} %bitcast.4) | data formatting | bytes 1310720
  74.0 0.0 copy-done.1
  74.0 0.0 copy-start
  74.0 0.7 copy.13
  74.7 0.5 copy-done
  75.2 0.0 copy-start.2
  75.2 0.8 %copy.14 = f32[9,32,512]{2,1,0:T(8,128)} copy(f32[9,32,512]{2,1,0:T(8,128)S(1)} %copy-done) | data formatting | bytes 1179648
  76.0 0.3 copy-done.2
  76.3 0.7 copy.15
Async XLA Ops:
  72.0 2.0 %copy-start.1 = (bf16[2,160,512]{2,1,0:T(8,128)(2,1)S(1)}, bf16[2,160,512]{2,1,0:T(8,128)(2,1)}, u32[]{:S(2)}) copy-start(bf16[2,160,512]{2,1,0:T(8,128)(2,1)} %get-tuple-element.9) | copy-start | bytes 983044
  74.0 1.2 %copy-start = (f32[9,32,512]{2,1,0:T(8,128)S(1)}, f32[9,32,512]{2,1,0:T(8,128)}, u32[]{:S(2)}) copy-start(f32[9,32,512]{2,1,0:T(8,128)} %get-tuple-element.18) | copy-start | bytes 1769476
  75.2 1.1 %copy-start.2 = (f32[3,32,512]{2,1,0:T(8,128)S(1)}, f32[3,32,512]{2,1,0:T(8,128)}, u32[]{:S(2)}) copy-start(f32[3,32,512]{2,1,0:T(8,128)} %get-tuple-element.19) | copy-start | bytes 589828

commit v6 on v4

--- a/solution.py
+++ b/solution.py
@@ -420,10 +420,13 @@
             fill_columns(
                 columns, width + frame * stride, value / (1.0 + jnp.exp(-value)), width, False
             )
+        columns_t[...] = columns[...].T
+
+    def lay_out_grads():
+        for frame in range(frames):
             place = slice((frame + 1) * pixels, (frame + 2) * pixels)
             even_ref[place] = c_all[frame // own, frame % own, 0]
             odd_ref[place] = c_all[frame // own, frame % own, 1]
-        columns_t[...] = columns[...].T
 
     def temporal_back():
         even = even_ref[pixels : (frames + 1) * pixels]
@@ -545,21 +548,22 @@
     relay_rows(0)
     for copy in kept:
         copy.wait()
-    for copy in pairs:
-        copy.wait_recv()
+    pairs[0].wait_recv()
     lay_out()
+    pairs[1].wait_recv()
+    lay_out_grads()
     relay_line(2)
-    relay_rows(1)
     complete(0)
     temporal_back()
+    relay_rows(1)
     relay_line(3)
-    relay_rows(2)
     spatial_weight_grads()
     sum_core(0)
+    relay_rows(2)
+    sum_rows(0)
     complete(1)
     spatial_row(0)
     relay_rows(3)
-    sum_rows(0)
     complete(2)
     spatial_row(1)
     complete(3)

time: 74.9 us -> 72.2 us (0.964)
  Pallas kernels: 69.5 us -> 66.7 us
    pallas_call x1, Pallas kernels: 69.5 us -> 66.7 us  [section(): pl.pallas_call(functools.partial(section_kernel, rows, width), out_shape=...]
where the time goes in v6:
time: 72.2 us; the launch traced here: 71.9 us
  Pallas kernels  66.7 us (92%)
  other arithmetic  2.64 us (4%)
  local copies, waits for them, and re-layouts  1.89 us (3%)
    pallas_call x1, Pallas kernels, section(): pl.pallas_call(functools.partial(section_kernel, rows, width), out_shape=...  66.7 us
    mul x1, other arithmetic, paired_device(): grad_s.astype(jnp.float32) * inverse  1.94 us
    unnamed x8, local copies, waits for them, and re-layouts  1.89 us

profile of v6, /device:TPU:0, one launch (start us, length us, event | category | flops | bytes accessed | tf_op | source)
XLA Modules:
  0.0 71.9 jit_solution(1150996397610444464)
XLA Ops:
  0.6 66.7 %section.1 = (bf16[2,2,160,512]{3,2,1,0:T(8,128)(2,1)}, bf16[2,160,512]{2,1,0:T(8,128)(2,1)}, bf16[9,32,512]{2,1,0:T(8,128)(2,1)}, bf16[3,32,512]{2,1,0:T(8,128)(2,1)}) custom-call(bf16[3,32,512]{2,1,0:T(8,128)(2,1)} %wt_ref.1, bf16[9,32,512]{2,1,0:T(8,128)(2,1)} %ws_ref.1, bf16[2,160,512]{2,1,0:T(8,128)(2,1)} %bitcast.7, bf16[2,2,160,512]{3,2,1,0:T(8,128)(2,1)} %bitcast.6), custom_call_target="tpu_custom_call" | custom-call | flops 6710886400 | bytes 12582912 | tf_op jit(solution)/shard_map/section/pallas_call | solution.py:610
  67.3 0.0 copy-start
  67.3 0.0 copy-start.2
  67.3 1.9 %convert_multiply_fusion = f32[9,32,512]{2,1,0:T(8,128)} fusion(bf16[9,32,512]{2,1,0:T(8,128)(2,1)} %get-tuple-element.10), kind=kLoop, calls=%fused_computation | loop fusion | flops 294912 | bytes 884736 | tf_op jit(solution)/shard_map/mul | solution.py:688
  69.3 0.0 copy-done.2
  69.3 0.7 convert_multiply_fusion.1
  70.0 0.0 copy-done
  70.0 0.0 copy-start.1
  70.0 0.8 %copy.10 = bf16[1,4,10,16,512]{4,3,2,1,0:T(8,128)(2,1)} copy(bf16[1,4,10,16,512]{4,3,2,1,0:T(8,128)(2,1)S(1)} %bitcast.4) | data formatting | bytes 1310720
  70.8 0.3 copy-done.1
  71.1 0.7 %copy.11 = bf16[1,2,10,16,512]{4,3,2,1,0:T(8,128)(2,1)} copy(bf16[1,2,10,16,512]{4,3,2,1,0:T(8,128)(2,1)S(1)} %bitcast.5) | data formatting | bytes 655360
Async XLA Ops:
  67.3 2.7 %copy-start = (bf16[2,2,160,512]{3,2,1,0:T(8,128)(2,1)S(1)}, bf16[2,2,160,512]{3,2,1,0:T(8,128)(2,1)}, u32[]{:S(2)}) copy-start(bf16[2,2,160,512]{3,2,1,0:T(8,128)(2,1)} %get-tuple-element.8) | copy-start | bytes 1966084
  67.3 2.0 %copy-start.2 = (bf16[3,32,512]{2,1,0:T(8,128)(2,1)S(1)}, bf16[3,32,512]{2,1,0:T(8,128)(2,1)}, u32[]{:S(2)}) copy-start(bf16[3,32,512]{2,1,0:T(8,128)(2,1)} %get-tuple-element.11) | copy-start | bytes 294916
  70.0 1.2 %copy-start.1 = (bf16[2,160,512]{2,1,0:T(8,128)(2,1)S(1)}, bf16[2,160,512]{2,1,0:T(8,128)(2,1)}, u32[]{:S(2)}) copy-start(bf16[2,160,512]{2,1,0:T(8,128)(2,1)} %get-tuple-element.9) | copy-start | bytes 983044

commit v7 on v6

--- a/solution.py
+++ b/solution.py
@@ -552,15 +552,15 @@
     lay_out()
     pairs[1].wait_recv()
     lay_out_grads()
-    relay_line(2)
     complete(0)
     temporal_back()
+    relay_line(2)
+    spatial_weight_grads()
+    sum_core(0)
     relay_rows(1)
     relay_line(3)
-    spatial_weight_grads()
-    sum_core(0)
+    sum_rows(0)
     relay_rows(2)
-    sum_rows(0)
     complete(1)
     spatial_row(0)
     relay_rows(3)

time: 72.2 us -> 75.2 us (1.042)
  Pallas kernels: 66.7 us -> 69.8 us
    pallas_call x1, Pallas kernels: 66.7 us -> 69.8 us  [section(): pl.pallas_call(functools.partial(section_kernel, rows, width), out_shape=...]
where the time goes in v7:
time: 75.2 us; the launch traced here: 75 us
  Pallas kernels  69.8 us (93%)
  other arithmetic  2.64 us (4%)
  local copies, waits for them, and re-layouts  1.89 us (3%)
    pallas_call x1, Pallas kernels, section(): pl.pallas_call(functools.partial(section_kernel, rows, width), out_shape=...  69.8 us
    mul x1, other arithmetic, paired_device(): grad_s.astype(jnp.float32) * inverse  1.94 us
    unnamed x8, local copies, waits for them, and re-layouts  1.89 us

profile of v7, /device:TPU:0, one launch (start us, length us, event | category | flops | bytes accessed | tf_op | source)
XLA Modules:
  0.0 75.0 jit_solution(7995655144647833084)
XLA Ops:
  0.6 69.8 %section.1 = (bf16[2,2,160,512]{3,2,1,0:T(8,128)(2,1)}, bf16[2,160,512]{2,1,0:T(8,128)(2,1)}, bf16[9,32,512]{2,1,0:T(8,128)(2,1)}, bf16[3,32,512]{2,1,0:T(8,128)(2,1)}) custom-call(bf16[3,32,512]{2,1,0:T(8,128)(2,1)} %wt_ref.1, bf16[9,32,512]{2,1,0:T(8,128)(2,1)} %ws_ref.1, bf16[2,160,512]{2,1,0:T(8,128)(2,1)} %bitcast.7, bf16[2,2,160,512]{3,2,1,0:T(8,128)(2,1)} %bitcast.6), custom_call_target="tpu_custom_call" | custom-call | flops 6710886400 | bytes 12582912 | tf_op jit(solution)/shard_map/section/pallas_call | solution.py:610
  70.5 0.0 copy-start
  70.5 0.0 copy-start.2
  70.5 1.9 %convert_multiply_fusion = f32[9,32,512]{2,1,0:T(8,128)} fusion(bf16[9,32,512]{2,1,0:T(8,128)(2,1)} %get-tuple-element.10), kind=kLoop, calls=%fused_computation | loop fusion | flops 294912 | bytes 884736 | tf_op jit(solution)/shard_map/mul | solution.py:688
  72.4 0.0 copy-done.2
  72.4 0.7 convert_multiply_fusion.1
  73.1 0.0 copy-done
  73.1 0.0 copy-start.1
  73.1 0.8 %copy.10 = bf16[1,4,10,16,512]{4,3,2,1,0:T(8,128)(2,1)} copy(bf16[1,4,10,16,512]{4,3,2,1,0:T(8,128)(2,1)S(1)} %bitcast.4) | data formatting | bytes 1310720
  74.0 0.3 copy-done.1
  74.3 0.7 copy.11
Async XLA Ops:
  70.5 2.7 %copy-start = (bf16[2,2,160,512]{3,2,1,0:T(8,128)(2,1)S(1)}, bf16[2,2,160,512]{3,2,1,0:T(8,128)(2,1)}, u32[]{:S(2)}) copy-start(bf16[2,2,160,512]{3,2,1,0:T(8,128)(2,1)} %get-tuple-element.8) | copy-start | bytes 1966084
  70.5 2.0 %copy-start.2 = (bf16[3,32,512]{2,1,0:T(8,128)(2,1)S(1)}, bf16[3,32,512]{2,1,0:T(8,128)(2,1)}, u32[]{:S(2)}) copy-start(bf16[3,32,512]{2,1,0:T(8,128)(2,1)} %get-tuple-element.11) | copy-start | bytes 294916
  73.1 1.2 %copy-start.1 = (bf16[2,160,512]{2,1,0:T(8,128)(2,1)S(1)}, bf16[2,160,512]{2,1,0:T(8,128)(2,1)}, u32[]{:S(2)}) copy-start(bf16[2,160,512]{2,1,0:T(8,128)(2,1)} %get-tuple-element.9) | copy-start | bytes 983044
